TPU v7x, 128 devices: a whole 4x4x4 slice. The times are simulated.
128 devices in a mesh: lat: 32 (over y, x_hi, z), lon: 2 (over x_lo), section: 2 (over core).
Axes of the slice: x: 4 (x_hi: 2, x_lo: 2; x = x_hi * 2 + x_lo), y: 4, z: 4, core: 2. Of those that a mesh axis runs over, the one named last changes fastest.
Arguments:
- boundary: bfloat16 [2, 2, 2, 192, 24, 1024], P('section', None, None, 'lat', 'lon'), may hold values from -6 to 6
- tile_kinds: int32 [2, 32, 2], P('section', 'lat', 'lon'), may hold values from 0 to 3
- proj_in: bfloat16 [2, 1024, 3072], P('section'), may hold values from -0.1875 to 0.1875
- proj_out: bfloat16 [2, 1024, 1024], P('section'), may hold values from -0.375 to 0.375
- offset_bias: float32 [2, 16, 759], P('section'), may hold values from -4 to 250
Outputs:
- boundary_out: bfloat16 [2, 2, 2, 192, 24, 1024], P('section', None, None, 'lat', 'lon')
- weight_grads: float32 [2, 1024, 4096], P('section', ('lat', 'lon'))
- bias_grads: float32 [2, 16, 759], P('section')
All inputs are finite; a program needn't handle non-finite values.
Results may differ from a plain program's by a relative error of at most 0.025.
Values may be sent and summed in bfloat16 or wider, within the bound.
No kernel may reach another device: no remote copies, remote signals or barrier semaphores. Data moves between devices by JAX's collectives and lax.ppermute only.
A program may use at most 192 MiB of HBM per device.

v0:
```python
import jax
import jax.numpy as jnp
from jax import lax
from jax.sharding import PartitionSpec as P

HEADS = 16
HEAD_DIM = 64
LEV = 2
WIN_LAT = 6
WIN_LON = 12
WT = 144


NORM_EPS = 1e-05
MASKED = -1e30


def shifted_2(shard, axis, by):
    size = lax.axis_size(axis)
    return lax.ppermute(shard, axis, [(i, (i + by) % size) for i in range(size)])


def from_behind(value, axis, steps):
    count = lax.axis_size(axis)
    leading, last = (max(0, -steps), min(count, count - steps))
    return lax.ppermute(value, axis, [(source, source + steps) for source in range(leading, last)])


def normed(volume):
    values = volume.astype(jnp.float32)
    average = jnp.mean(values, axis=-1, keepdims=True)
    centered = values - average
    variance = jnp.mean(centered * centered, axis=-1, keepdims=True)
    return (centered * lax.rsqrt(variance + NORM_EPS)).astype(jnp.bfloat16)


def to_windows(volume):
    micro_count, levels, lat_rows, lon_cols, features = volume.shape
    pieces = volume.reshape(
        micro_count, levels, lat_rows // WIN_LAT, WIN_LAT, lon_cols // WIN_LON, WIN_LON, features
    )
    pieces = pieces.transpose(0, 2, 4, 1, 3, 5, 6)
    return pieces.reshape(-1, levels * WIN_LAT * WIN_LON, features)


def from_windows(windows, shape):
    micro_count, levels, lat_rows, lon_cols = shape
    features = windows.shape[-1]
    pieces = windows.reshape(
        micro_count, lat_rows // WIN_LAT, lon_cols // WIN_LON, levels, WIN_LAT, WIN_LON, features
    )
    pieces = pieces.transpose(0, 3, 1, 4, 2, 5, 6)
    return pieces.reshape(micro_count, levels, lat_rows, lon_cols, features)


def offset_table(count):
    spots = jnp.arange(count)
    distance = spots[:, None] - spots[None, :] + (count - 1)
    return (distance[:, :, None] == jnp.arange(2 * count - 1)[None, None, :]).astype(jnp.float32)


def pair_bias(table):
    heads = table.shape[0]
    cube = table.reshape(heads, 2 * LEV - 1, 2 * WIN_LAT - 1, 2 * WIN_LON - 1)
    exact = lax.Precision.HIGHEST
    along_cols = jnp.einsum("hxyz,cdz->hxycd", cube, offset_table(WIN_LON), precision=exact)
    along_rows = jnp.einsum("hxycd,aby->hxabcd", along_cols, offset_table(WIN_LAT), precision=exact)
    along_levels = jnp.einsum("hxabcd,efx->heacfbd", along_rows, offset_table(LEV), precision=exact)
    return along_levels.reshape(heads, WT, WT)


def attend(projected, bias_full, allowed):
    window_count, window_len = (projected.shape[0], projected.shape[1])
    pieces = projected.reshape(window_count, window_len, 3, HEADS, HEAD_DIM)
    queries, key_part, value_part = (pieces[:, :, 0], pieces[:, :, 1], pieces[:, :, 2])
    scores = jnp.einsum(
        "wqhd,wkhd->whqk", queries, key_part, preferred_element_type=jnp.float32
    ) * HEAD_DIM ** (-0.5)
    scores = jnp.where(allowed[:, None], scores + bias_full[None], MASKED)
    peak = lax.stop_gradient(jnp.max(scores, axis=-1, keepdims=True))
    weights = jnp.exp(scores - peak)
    chances = (weights / jnp.sum(weights, axis=-1, keepdims=True)).astype(jnp.bfloat16)
    context = jnp.einsum("whqk,wkhd->wqhd", chances, value_part, preferred_element_type=jnp.float32)
    return context.reshape(window_count, window_len, HEADS * HEAD_DIM).astype(jnp.bfloat16)


def move_lat(volume, step_by):
    return shifted_2(volume, "lat", step_by)


def move_lon(volume, step_by):
    return shifted_2(volume, "lon", step_by)


def roll_forward(volume):
    half_lat = WIN_LAT // 2
    half_lon = WIN_LON // 2
    arrived = move_lat(volume[:, :, :half_lat], -1)
    partway = jnp.concatenate([volume[:, :, half_lat:], arrived], axis=2)
    arrived_cols = move_lon(partway[:, :, :, :half_lon], -1)
    return jnp.concatenate([partway[:, :, :, half_lon:], arrived_cols], axis=3)


def roll_backward(volume):
    half_lat = WIN_LAT // 2
    half_lon = WIN_LON // 2
    arrived_cols = move_lon(volume[:, :, :, -half_lon:], 1)
    partway = jnp.concatenate([arrived_cols, volume[:, :, :, :-half_lon]], axis=3)
    arrived = move_lat(partway[:, :, -half_lat:], 1)
    return jnp.concatenate([arrived, partway[:, :, :-half_lat]], axis=2)


def weight_terms(blocks):
    normal_flat, grad_proj, context, grad_flat = blocks
    into = lax.dot_general(
        normal_flat, grad_proj, (((0,), (0,)), ((), ())), preferred_element_type=jnp.float32
    )
    outof = lax.dot_general(
        context, grad_flat, (((0,), (0,)), ((), ())), preferred_element_type=jnp.float32
    )
    return lax.psum_scatter(
        jnp.concatenate([into, outof], axis=1), ("lat", "lon"), scatter_dimension=0, tiled=True
    )


def per_device(boundary, tile_kinds, proj_in, proj_out, offset_bias):
    section_id = lax.axis_index("section")
    is_first = section_id == 0
    shifted = section_id == 1
    proj_one = proj_in[0]
    proj_two = proj_out[0]
    bias_table = offset_bias[0]
    bias_full, bias_back = jax.vjp(pair_bias, bias_table)
    kinds_flat = tile_kinds[0].reshape(-1)
    micro_total = boundary.shape[1]
    lat_rows = boundary.shape[3]
    lon_cols = boundary.shape[4]
    batch_rows = boundary.shape[2] * lat_rows * lon_cols
    token = jnp.arange(WT)
    low_row = token // WIN_LON % WIN_LAT < WIN_LAT // 2
    low_col = token % WIN_LON < WIN_LON // 2
    row_same = low_row[:, None] == low_row[None, :]
    col_same = low_col[:, None] == low_col[None, :]

    def window_mask(micro_count):
        split_rows = jnp.tile(kinds_flat % 2 == 1, micro_count)[:, None, None]
        split_cols = jnp.tile(kinds_flat // 2 == 1, micro_count)[:, None, None]
        return (row_same[None] | ~split_rows) & (col_same[None] | ~split_cols)

    def forward(volume):
        allowed = window_mask(volume.shape[0])
        moved = jnp.where(shifted, roll_forward(volume), volume)
        features = moved.shape[-1]
        normal_flat = normed(moved).reshape(-1, features)
        projected = jnp.dot(normal_flat, proj_one, preferred_element_type=jnp.float32).astype(
            jnp.bfloat16
        )
        windows = to_windows(projected.reshape(moved.shape[:4] + (3 * features,)))
        context = from_windows(attend(windows, bias_full, allowed), moved.shape[:4]).reshape(
            -1, features
        )
        mixed = jnp.dot(context, proj_two, preferred_element_type=jnp.float32)
        result = (
            (moved.reshape(-1, features).astype(jnp.float32) + mixed)
            .astype(jnp.bfloat16)
            .reshape(moved.shape)
        )
        output = jnp.where(shifted, roll_backward(result), result)
        return (output, (moved, normal_flat, windows, context))

    def backward(saved, cotangent):
        moved, normal_flat, windows, context = saved
        features = moved.shape[-1]
        allowed = window_mask(moved.shape[0])
        grad_out = jnp.where(shifted, roll_forward(cotangent), cotangent)
        unused, norm_back = jax.vjp(normed, moved)

        def attend_open(part_in, bias_in):
            return attend(part_in, bias_in, allowed)

        again, attend_back = jax.vjp(attend_open, windows, bias_full)
        grad_flat = grad_out.reshape(-1, features)
        grad_context = lax.dot_general(
            grad_flat, proj_two, (((1,), (1,)), ((), ())), preferred_element_type=jnp.float32
        ).astype(jnp.bfloat16)
        grad_windows, grad_pair = attend_back(to_windows(grad_context.reshape(moved.shape)))
        grad_proj = from_windows(grad_windows, moved.shape[:4]).reshape(-1, 3 * features)
        grad_normal = lax.dot_general(
            grad_proj, proj_one, (((1,), (1,)), ((), ())), preferred_element_type=jnp.float32
        ).astype(jnp.bfloat16)
        grad_norm_in = norm_back(grad_normal.reshape(moved.shape))[0]
        grad_moved = (grad_out.astype(jnp.float32) + grad_norm_in.astype(jnp.float32)).astype(
            jnp.bfloat16
        )
        grad_in = jnp.where(shifted, roll_backward(grad_moved), grad_moved)
        return (grad_in, (normal_flat, grad_proj, context, grad_flat), grad_pair)

    def per_micro(parts, micro):
        return tuple((piece[micro * batch_rows : (micro + 1) * batch_rows] for piece in parts))

    first_in = jnp.where(is_first, boundary[0], jnp.zeros_like(boundary[0]))
    out_first, saved_first = forward(first_in)
    received = from_behind(out_first, "section", 1)
    out_second, saved_second = forward(received)
    cot_second = jnp.where(shifted, boundary[0], jnp.zeros_like(boundary[0]))
    grad_second, rows_second, pair_second = backward(saved_second, cot_second)
    grad_received = from_behind(grad_second, "section", -1)
    grad_firsts, rows_first, pair_first = backward(saved_first, grad_received)
    result = jnp.where(is_first, grad_firsts, out_second)
    chosen = tuple(
        (
            jnp.where(is_first, left_part, right_part)
            for left_part, right_part in zip(rows_first, rows_second)
        )
    )
    blocks = [per_micro(chosen, micro) for micro in range(micro_total)]
    pair_total = pair_first + pair_second
    merged = tuple(
        (jnp.concatenate([block[member] for block in blocks], axis=0) for member in range(4))
    )
    grad_rows = weight_terms(merged)
    bias_total = bias_back(pair_total)[0]
    bias_sum = lax.psum(bias_total, ("lat", "lon"))
    return (result[None], grad_rows[None], bias_sum[None])


def solution(mesh):
    return jax.shard_map(
        per_device,
        mesh=mesh,
        in_specs=(
            P("section", None, None, "lat", "lon", None),
            P("section", "lat", "lon"),
            P("section", None, None),
            P("section", None, None),
            P("section", None, None),
        ),
        out_specs=(
            P("section", None, None, "lat", "lon", None),
            P("section", ("lat", "lon"), None),
            P("section", None, None),
        ),
        check_vma=False,
    )
```

profile of v0, /device:TPU:0, one launch (start us, length us, event | category | flops | bytes accessed | tf_op | source)
XLA Modules:
  0.0 940.7 jit_solution(4278692716062272198)
XLA Ops:
  10.4 9.0 collective-permute-start.2
  30.4 17.4 %convolution_bitcast_fusion = f32[16,3,6,6,12,12]{0,3,5,4,1,2:T(8,128)S(1)} fusion(f32[16,3,11,12,12]{2,0,4,3,1:T(8,128)} %copy.75, s32[6,6]{1,0:T(8,128)S(1)} %subtract_add_fusion.1), kind=kOutput, calls=%fused_computation.50 | convolution fusion | flops 32846220 | bytes 1299600 | tf_op jit(solution)/shard_map/jvp(hxycd,aby->hxabcd)/dot_general | solution.py:67
  47.8 20.7 %fusion.10 = f32[16,2,6,12,2,6,12]{0,4,6,3,5,2,1:T(2,128)} fusion(f32[16,3,6,6,12,12]{0,3,5,4,1,2:T(8,128)S(1)} %convolution_bitcast_fusion, s32[2,2]{1,0:T(2,128)S(1)} %subtract_add_fusion.2), kind=kOutput, calls=%fused_computation.9 | convolution fusion | flops 11943948 | bytes 2322448 | tf_op jit(solution)/shard_map/jvp(hxabcd,efx->heacfbd)/dot_general | solution.py:68
  70.2 26.3 %copy.134 = f32[16,2,6,12,2,6,12]{3,2,1,6,5,4,0:T(8,128)} copy(f32[16,2,6,12,2,6,12]{0,4,6,3,5,2,1:T(2,128)} %fusion.10) | data formatting | bytes 2654208 | tf_op jit(solution)/shard_map/add | solution.py:79
  96.5 13.4 %reshape.451 = f32[16,144,144]{1,2,0:T(8,128)} reshape(f32[16,2,6,12,2,6,12]{3,2,1,6,5,4,0:T(8,128)} %copy.134) | data formatting | bytes 2654208 | tf_op jit(solution)/shard_map/add | solution.py:79
  112.6 9.2 collective-permute-done.3
  166.9 9.1 collective-permute-done.4
  176.7 14.4 %collective-permute-done.5 = bf16[2,2,3,12,1024]{4,3,2,1,0:T(8,128)(2,1)S(1)} collective-permute-done((bf16[2,2,3,12,1024]{4,3,2,1,0:T(8,128)(2,1)S(1)}, bf16[2,2,3,12,1024]{4,3,2,1,0:T(8,128)(2,1)S(1)}, u32[]{:S(2)}, u32[]{:S(2)}) %collective-permute-start.5) | collective-permute-done | bytes 294944 | tf_op jit(solution)/shard_map/ppermute | solution.py:20
  193.6 7.8 collective-permute-done
  204.2 7.0 collective-permute-start.7
  273.7 6.6 copy.93
  298.9 7.1 collective-permute-done.9
  306.2 16.8 %collective-permute-done.10 = bf16[2,2,3,12,1024]{4,3,2,1,0:T(8,128)(2,1)S(1)} collective-permute-done((bf16[2,2,3,12,1024]{4,3,2,1,0:T(8,128)(2,1)S(1)}, bf16[2,2,3,12,1024]{4,3,2,1,0:T(8,128)(2,1)S(1)}, u32[]{:S(2)}, u32[]{:S(2)}) %collective-permute-start.10) | collective-permute-done | bytes 294944 | tf_op jit(solution)/shard_map/ppermute | solution.py:20
  334.8 6.7 collective-permute-done.12
  387.8 6.6 copy.106
  422.1 17.2 %collective-permute-done.16 = bf16[2,2,6,6,1024]{4,3,2,1,0:T(8,128)(2,1)} collective-permute-done((bf16[2,2,6,6,1024]{4,3,2,1,0:T(8,128)(2,1)}, bf16[2,2,6,6,1024]{4,3,2,1,0:T(8,128)(2,1)}, u32[]{:S(2)}, u32[]{:S(2)}) %collective-permute-start.16) | collective-permute-done | bytes 294944 | tf_op jit(solution)/shard_map/ppermute | solution.py:20
  441.1 7.2 fusion.207
  453.5 6.7 copy.103
  465.9 6.4 fusion.127
  483.0 13.2 %add.188 = f32[16,2,6,12,2,6,12]{6,5,4,3,2,1,0:T(8,128)} reshape(f32[16,144,144]{2,1,0:T(8,128)} %copy.109) | data formatting | bytes 2654208 | tf_op jit(solution)/shard_map/add | solution.py:217
  496.2 41.4 %fusion.7 = f32[6,6,16,3,12,12]{5,3,4,1,0,2:T(4,128)} fusion(f32[2,2,16,6,6,12,12]{6,4,1,5,3,0,2:T(8,128)} %bitcast.216, s32[2,2]{1,0:T(2,128)S(1)} %copy-done.58), kind=kOutput, calls=%fused_computation.8 | convolution fusion | flops 11943948 | bytes 2322448 | tf_op jit(solution)/shard_map/transpose(jvp(hxabcd,efx->heacfbd))/dot_general | solution.py:68
  537.6 20.7 %copy.111 = f32[6,6,16,3,12,12]{2,1,0,5,4,3:T(8,128)} copy(f32[6,6,16,3,12,12]{5,3,4,1,0,2:T(4,128)} %fusion.7) | data formatting | bytes 1990656 | tf_op jit(solution)/shard_map/transpose(jvp(hxycd,aby->hxabcd))/transpose;transpose(jvp(hxabcd,efx->heacfbd))/transpose | solution.py:67
  558.4 9.9 %convolution_bitcast_fusion.1 = f32[16,3,11,12,12]{2,0,4,3,1:T(8,128)S(1)} fusion(f32[6,6,16,3,12,12]{2,1,0,5,4,3:T(8,128)} %copy.111, s32[6,6]{1,0:T(8,128)S(1)} %copy-done.46), kind=kOutput, calls=%fused_computation.79 | convolution fusion | flops 32846220 | bytes 1299600 | tf_op jit(solution)/shard_map/transpose(jvp(hxycd,aby->hxabcd))/dot_general | solution.py:67
  576.2 353.5 %psum.7 = f32[1,16,759]{2,1,0:T(8,128)} all-reduce(f32[1,16,759]{2,1,0:T(8,128)S(1)} %broadcast_in_dim.142), channel_id=1, replica_groups=mesh['lat'=32,'lon'=2,'section'=2] {'lat','lon'}, use_global_device_ids=true, to_apply=%region_17.18 | all-reduce | flops 12144 | bytes 97152 | tf_op jit(solution)/shard_map/psum | solution.py:223
  (287 shorter events, 270.3 us)
Async XLA Ops:
  7.2 156.7 %copy-start = (bf16[1,1024,1024]{2,1,0:T(8,128)(2,1)S(1)}, bf16[1,1024,1024]{2,1,0:T(8,128)(2,1)}, u32[]{:S(2)}) copy-start(bf16[1,1024,1024]{2,1,0:T(8,128)(2,1)} %param.8) | copy-start | bytes 6291460
  7.2 926.2 %reduce-scatter.2.cloned.1.call-start = ((), (), s32[]{:S(2)}) async-start(), calls=%async_computation.1 | async-start | bytes 17039360 | tf_op jit(solution)/shard_map/reduce_scatter | solution.py:121
  10.4 99.5 %collective-permute-start.2 = (bf16[2,2,3,12,1024]{4,3,2,1,0:T(8,128)(2,1)}, bf16[2,2,3,12,1024]{4,3,2,1,0:T(8,128)(2,1)}, u32[]{:S(2)}, u32[]{:S(2)}) collective-permute-start(bf16[2,2,3,12,1024]{4,3,2,1,0:T(8,128)(2,1)} %get-tuple-element.48), channel_id=1, source_target_pairs={{0,124},{4,0},{8,4},{12,8},{16,12},{20,16},{24,20},{28,24},{32,28}... | collective-permute-start | bytes 884744 | tf_op jit(solution)/shard_map/ppermute | solution.py:20
  19.5 28.4 %copy-start.57 = (s32[2,2]{1,0:T(2,128)}, s32[2,2]{1,0:T(2,128)S(1)}, u32[]{:S(2)}) copy-start(s32[2,2]{1,0:T(2,128)S(1)} %subtract_add_fusion.2) | copy-start | bytes 52
  111.2 10.6 %collective-permute-start.3 = (bf16[2,2,6,6,1024]{4,3,2,1,0:T(8,128)(2,1)S(1)}, bf16[2,2,6,6,1024]{4,3,2,1,0:T(8,128)(2,1)S(1)}, u32[]{:S(2)}, u32[]{:S(2)}) collective-permute-start(bf16[2,2,6,6,1024]{4,3,2,1,0:T(8,128)(2,1)S(1)} %get-tuple-element.46), channel_id=1, source_target_pairs={{0,2},{2,0},{1,3},{3,1},{4,6},{6,4},{5,7},{7,5},{8,10},{10,8},{9,1... | collective-permute-start | bytes 884744 | tf_op jit(solution)/shard_map/ppermute | solution.py:20
  166.2 9.7 %collective-permute-start.4 = (bf16[2,2,6,6,1024]{4,3,2,1,0:T(8,128)(2,1)S(1)}, bf16[2,2,6,6,1024]{4,3,2,1,0:T(8,128)(2,1)S(1)}, u32[]{:S(2)}, u32[]{:S(2)}) collective-permute-start(bf16[2,2,6,6,1024]{4,3,2,1,0:T(8,128)(2,1)S(1)} %get-tuple-element.43), channel_id=1, source_target_pairs={{0,2},{2,0},{1,3},{3,1},{4,6},{6,4},{5,7},{7,5},{8,10},{10,8},{9,1... | collective-permute-start | bytes 884744 | tf_op jit(solution)/shard_map/ppermute | solution.py:20
  176.1 15.0 %collective-permute-start.5 = (bf16[2,2,3,12,1024]{4,3,2,1,0:T(8,128)(2,1)S(1)}, bf16[2,2,3,12,1024]{4,3,2,1,0:T(8,128)(2,1)S(1)}, u32[]{:S(2)}, u32[]{:S(2)}) collective-permute-start(bf16[2,2,3,12,1024]{4,3,2,1,0:T(8,128)(2,1)S(1)} %fusion.166), channel_id=1, source_target_pairs={{0,4},{4,8},{8,12},{12,16},{16,20},{20,24},{24,28},{28,32},{32,36}... | collective-permute-start | bytes 884744 | tf_op jit(solution)/shard_map/ppermute | solution.py:20
  192.1 10.1 %collective-permute-start.6 = (bf16[2,2,6,12,1024]{4,1,3,2,0:T(2,128)(2,1)S(1)}, bf16[2,2,6,12,1024]{4,1,3,2,0:T(2,128)(2,1)S(1)}, u32[]{:S(2)}, u32[]{:S(2)}) collective-permute-start(bf16[2,2,6,12,1024]{4,1,3,2,0:T(2,128)(2,1)S(1)} %copy.81), channel_id=1, source_target_pairs={{0,1},{2,3},{4,5},{6,7},{8,9},{10,11},{12,13},{14,15},{16,17},{18,... | collective-permute-start | bytes 1769480 | tf_op jit(solution)/shard_map/ppermute | solution.py:26
  193.5 7.9 collective-permute-start
  201.5 9.7 %collective-permute-start.1 = (bf16[2,2,6,6,1024]{4,3,2,1,0:T(8,128)(2,1)S(1)}, bf16[2,2,6,6,1024]{4,3,2,1,0:T(8,128)(2,1)S(1)}, u32[]{:S(2)}, u32[]{:S(2)}) collective-permute-start(bf16[2,2,6,6,1024]{4,3,2,1,0:T(8,128)(2,1)S(1)} %get-tuple-element.36), channel_id=1, source_target_pairs={{0,2},{2,0},{1,3},{3,1},{4,6},{6,4},{5,7},{7,5},{8,10},{10,8},{9,1... | collective-permute-start | bytes 884744 | tf_op jit(solution)/shard_map/ppermute | solution.py:20
  204.2 13.5 %collective-permute-start.7 = (bf16[2,2,3,12,1024]{4,3,2,1,0:T(8,128)(2,1)}, bf16[2,2,3,12,1024]{4,3,2,1,0:T(8,128)(2,1)}, u32[]{:S(2)}, u32[]{:S(2)}) collective-permute-start(bf16[2,2,3,12,1024]{4,3,2,1,0:T(8,128)(2,1)} %copy.174), channel_id=1, source_target_pairs={{0,124},{4,0},{8,4},{12,8},{16,12},{20,16},{24,20},{28,24},{32,28}... | collective-permute-start | bytes 884744 | tf_op jit(solution)/shard_map/ppermute | solution.py:20
  219.8 9.5 %collective-permute-start.8 = (bf16[2,2,6,6,1024]{4,3,2,1,0:T(8,128)(2,1)}, bf16[2,2,6,6,1024]{4,3,2,1,0:T(8,128)(2,1)}, u32[]{:S(2)}, u32[]{:S(2)}) collective-permute-start(bf16[2,2,6,6,1024]{4,3,2,1,0:T(8,128)(2,1)} %get-tuple-element.42), channel_id=1, source_target_pairs={{0,2},{2,0},{1,3},{3,1},{4,6},{6,4},{5,7},{7,5},{8,10},{10,8},{9,1... | collective-permute-start | bytes 884744 | tf_op jit(solution)/shard_map/ppermute | solution.py:20
  298.2 7.9 collective-permute-start.9
  306.2 16.9 %collective-permute-start.10 = (bf16[2,2,3,12,1024]{4,3,2,1,0:T(8,128)(2,1)S(1)}, bf16[2,2,3,12,1024]{4,3,2,1,0:T(8,128)(2,1)S(1)}, u32[]{:S(2)}, u32[]{:S(2)}) collective-permute-start(bf16[2,2,3,12,1024]{4,3,2,1,0:T(8,128)(2,1)S(1)} %fusion.164), channel_id=1, source_target_pairs={{0,4},{4,8},{8,12},{12,16},{16,20},{20,24},{24,28},{28,32},{32,36}... | collective-permute-start | bytes 884744 | tf_op jit(solution)/shard_map/ppermute | solution.py:20
  324.0 3.9 collective-permute-start.11
  330.1 11.5 %collective-permute-start.12 = (bf16[2,2,3,12,1024]{4,3,2,1,0:T(8,128)(2,1)}, bf16[2,2,3,12,1024]{4,3,2,1,0:T(8,128)(2,1)}, u32[]{:S(2)}, u32[]{:S(2)}) collective-permute-start(bf16[2,2,3,12,1024]{4,3,2,1,0:T(8,128)(2,1)} %copy.176), channel_id=1, source_target_pairs={{0,124},{4,0},{8,4},{12,8},{16,12},{20,16},{24,20},{28,24},{32,28}... | collective-permute-start | bytes 884744 | tf_op jit(solution)/shard_map/ppermute | solution.py:20
  343.6 10.6 %collective-permute-start.13 = (bf16[2,2,6,6,1024]{4,3,2,1,0:T(8,128)(2,1)}, bf16[2,2,6,6,1024]{4,3,2,1,0:T(8,128)(2,1)}, u32[]{:S(2)}, u32[]{:S(2)}) collective-permute-start(bf16[2,2,6,6,1024]{4,3,2,1,0:T(8,128)(2,1)} %get-tuple-element.32), channel_id=1, source_target_pairs={{0,2},{2,0},{1,3},{3,1},{4,6},{6,4},{5,7},{7,5},{8,10},{10,8},{9,1... | collective-permute-start | bytes 884744 | tf_op jit(solution)/shard_map/ppermute | solution.py:20
  419.9 28.4 %copy-start.15 = (bf16[2,2,6,12,1024]{4,3,2,1,0:T(8,128)(2,1)}, bf16[2,2,6,12,1024]{4,3,2,1,0:T(8,128)(2,1)S(1)}, u32[]{:S(2)}) copy-start(bf16[2,2,6,12,1024]{4,3,2,1,0:T(8,128)(2,1)S(1)} %reshape.436) | copy-start | bytes 1769476
  420.9 18.4 %collective-permute-start.16 = (bf16[2,2,6,6,1024]{4,3,2,1,0:T(8,128)(2,1)}, bf16[2,2,6,6,1024]{4,3,2,1,0:T(8,128)(2,1)}, u32[]{:S(2)}, u32[]{:S(2)}) collective-permute-start(bf16[2,2,6,6,1024]{4,3,2,1,0:T(8,128)(2,1)} %get-tuple-element.39), channel_id=1, source_target_pairs={{0,2},{2,0},{1,3},{3,1},{4,6},{6,4},{5,7},{7,5},{8,10},{10,8},{9,1... | collective-permute-start | bytes 884744 | tf_op jit(solution)/shard_map/ppermute | solution.py:20
  441.1 488.6 %collective-permute-start.17 = (bf16[2,2,3,12,1024]{4,3,2,1,0:T(8,128)(2,1)}, bf16[2,2,3,12,1024]{4,3,2,1,0:T(8,128)(2,1)}, u32[]{:S(2)}, u32[]{:S(2)}) collective-permute-start(bf16[2,2,3,12,1024]{4,3,2,1,0:T(8,128)(2,1)} %fusion.161), channel_id=1, source_target_pairs={{0,4},{4,8},{8,12},{12,16},{16,20},{20,24},{24,28},{28,32},{32,36}... | collective-permute-start | bytes 884744 | tf_op jit(solution)/shard_map/ppermute | solution.py:20
  483.0 85.3 %copy-start.31 = (bf16[2,2,6,6,1024]{4,3,2,1,0:T(8,128)(2,1)}, bf16[2,2,6,6,1024]{4,3,2,1,0:T(8,128)(2,1)S(1)}, u32[]{:S(2)}) copy-start(bf16[2,2,6,6,1024]{4,3,2,1,0:T(8,128)(2,1)S(1)} %get-tuple-element.30) | copy-start | bytes 884740
  483.0 85.2 %collective-permute-start.14 = (bf16[2,2,6,6,1024]{4,3,2,1,0:T(8,128)(2,1)}, bf16[2,2,6,6,1024]{4,3,2,1,0:T(8,128)(2,1)S(1)}, u32[]{:S(2)}, u32[]{:S(2)}) collective-permute-start(bf16[2,2,6,6,1024]{4,3,2,1,0:T(8,128)(2,1)} %get-tuple-element.29), channel_id=1, source_target_pairs={{0,2},{2,0},{1,3},{3,1},{4,6},{6,4},{5,7},{7,5},{8,10},{10,8},{9,1... | collective-permute-start | bytes 884744 | tf_op jit(solution)/shard_map/ppermute | solution.py:20
  569.9 359.8 %copy-start.16 = (bf16[2,2,6,12,1024]{4,3,2,1,0:T(8,128)(2,1)S(1)}, bf16[2,2,6,12,1024]{4,3,2,1,0:T(8,128)(2,1)}, u32[]{:S(2)}) copy-start(bf16[2,2,6,12,1024]{4,3,2,1,0:T(8,128)(2,1)} %copy-done.15) | copy-start | bytes 1769476
  569.9 359.8 %collective-permute-start.15 = (bf16[2,2,3,12,1024]{4,3,2,1,0:T(8,128)(2,1)}, bf16[2,2,3,12,1024]{4,3,2,1,0:T(8,128)(2,1)}, u32[]{:S(2)}, u32[]{:S(2)}) collective-permute-start(bf16[2,2,3,12,1024]{4,3,2,1,0:T(8,128)(2,1)} %fusion.162), channel_id=1, source_target_pairs={{0,4},{4,8},{8,12},{12,16},{16,20},{20,24},{24,28},{28,32},{32,36}... | collective-permute-start | bytes 884744 | tf_op jit(solution)/shard_map/ppermute | solution.py:20
  (56 other events, 362.2 us)
Sparse Core Ops, SparseCore 0:
  412.9 410.8 reduce-scatter.1
where the time goes:
time: 953 us; the launch traced here: 941 us
  blocking collectives  353 us (37%)
  local copies, waits for them, and re-layouts  219 us (23%)
  matrix products  168 us (18%)
  waiting for transfers between devices  95.8 us (10%)
  other arithmetic  60.4 us (6%)
  starting transfers between devices  28 us (3%)
  between operations  16.2 us (2%)
    psum x1, blocking collectives, per_device(): bias_sum = lax.psum(bias_total, ('lat', 'lon'))  353 us
    ppermute x16, waiting for transfers between devices, shifted_2(): lax.ppermute(shard, axis, [(i, (i + by) % size) for i in range(size)])  93.4 us
    dot_general x2, matrix products, pair_bias(): jnp.einsum('hxabcd,efx->heacfbd', along_rows, offset_table(LEV), precisio...  62.1 us
    add x2, local copies, waits for them, and re-layouts, attend(): scores = jnp.where(allowed[:, None], scores + bias_full[None], MASKED)  39.7 us
    unnamed x133, local copies, waits for them, and re-layouts  29.2 us
    dot_general x2, matrix products, pair_bias(): jnp.einsum('hxycd,aby->hxabcd', along_cols, offset_table(WIN_LAT), precis...  27.3 us
    ppermute x16, starting transfers between devices, shifted_2(): lax.ppermute(shard, axis, [(i, (i + by) % size) for i in range(size)])  25.1 us
    select_n x6, local copies, waits for them, and re-layouts, per_device(): jnp.where(is_first, left_part, right_part)  21.6 us
  transfers between devices with their start and end apart: 19, of which 11 were waited for; matrix products, arithmetic and copies ran while one was open for 28% of the time, Pallas kernels for 0%

commit v1 on v0

v1 whole, which is shorter than its diff:
```python
import functools

import jax
import jax.numpy as jnp
import numpy as np
from jax import lax
from jax.experimental import pallas as pl
from jax.experimental.pallas import tpu as pltpu
from jax.sharding import PartitionSpec as P

D = 1024
HEADS = 16
LEV = 2
MICRO = 2
WIN_LAT = 6
WIN_LON = 12
WT = 144
TOK = MICRO * WT
QT = TOK // 4
OFFSETS = 759
OPAD = 768
REACH = 384
PAIRS = HEADS // 2
GROUP = 4
BIAS_ROWS = 16
NORM_EPS = 1e-05
MASKED = -1e30
BF = jnp.bfloat16
F32 = jnp.float32
VLIMIT = 56 * 1024 * 1024

ANY = pl.BlockSpec(memory_space=pl.ANY)
VMEM = pl.BlockSpec(memory_space=pltpu.VMEM)
SMEM = pl.BlockSpec(memory_space=pltpu.SMEM)


def constants():
    tok = np.arange(WT)
    lev, row, col = tok // 72, tok // 12 % 6, tok % 12
    reach = 379 - (253 * lev + 23 * row + col)
    onehot = np.zeros((256, REACH), np.float32)
    onehot[tok, reach] = 1
    rows_differ = ((row < 3)[:, None] != (row < 3)[None, :]).astype(np.float32)
    cols_differ = ((col < 6)[:, None] != (col < 6)[None, :]).astype(np.float32)
    pick = np.zeros((4, QT, TOK), np.float32)
    for half_row in range(2):
        for half_col in range(2):
            at = 0
            for micro in range(MICRO):
                for level in range(LEV):
                    for r in range(3):
                        for c in range(6):
                            src = micro * WT + level * 72 + (3 * half_row + r) * 12 + 6 * half_col + c
                            pick[half_row * 2 + half_col, at, src] = 1
                            at += 1
    return onehot, rows_differ, cols_differ, pick


ONEHOT, ROWS_DIFFER, COLS_DIFFER, PICK = constants()
SHIFTS = [253 * (a // 6) + 23 * (a % 6) for a in range(12)]


def dot(a, b):
    return jnp.dot(a, b, preferred_element_type=F32)


def dot_nt(a, b):
    return lax.dot_general(a, b, (((1,), (1,)), ((), ())), preferred_element_type=F32)


def dot_tn(a, b):
    return lax.dot_general(a, b, (((0,), (0,)), ((), ())), preferred_element_type=F32)


def call(body, name, out_shape, in_specs, scratch, flops, nbytes):
    out_specs = jax.tree.map(lambda _: VMEM, out_shape)
    return pl.pallas_call(
        body,
        out_shape=out_shape,
        in_specs=in_specs,
        out_specs=out_specs,
        scratch_shapes=scratch,
        compiler_params=pltpu.CompilerParams(vmem_limit_bytes=VLIMIT),
        cost_estimate=pl.CostEstimate(flops=flops, bytes_accessed=nbytes, transcendentals=0),
        name=name,
    )


def shape(*dims, dtype=BF):
    return jax.ShapeDtypeStruct(dims, dtype)


def load_groups(x_ref, dst):
    for g in range(TOK // 12):
        dst[12 * g : 12 * g + 12, :] = x_ref[g].astype(F32)


def store_groups(src, out_ref):
    for g in range(TOK // 12):
        out_ref[g] = src[12 * g : 12 * g + 12, :].astype(BF)


def insert(piece_refs, pickt_ref):
    total = dot(pickt_ref[0], piece_refs[0][...])
    for q in range(1, 4):
        total = total + dot(pickt_ref[q], piece_refs[q][...])
    return total


def extract(value, pick_ref, out_refs):
    for q in range(4):
        out_refs[q][...] = dot(pick_ref[q], value).astype(BF)


def bias_body(who, kind, x_ref, table_ref, oht_ref, rdiff, cdiff, pick_ref, out_ref, c0, c1, c2, c3, xs, tab, wide, tall, edge):
    tab[...] = jnp.zeros_like(tab)
    tab[:, :OFFSETS] = table_ref[...]
    table = tab[...]
    for cq in range(12):
        near = table if cq == 0 else pltpu.roll(table, OPAD - cq, 1)
        for a in range(12):
            moved = near if SHIFTS[a] == 0 else pltpu.roll(near, OPAD - SHIFTS[a], 1)
            wide[(a * 12 + cq) * 16 : (a * 12 + cq) * 16 + 16, :] = moved[:, :REACH]
    for a in range(12):
        x = wide[a * 192 : a * 192 + 192, :]
        top = x.astype(BF)
        rest = x - top.astype(F32)
        middle = rest.astype(BF)
        low = (rest - middle.astype(F32)).astype(BF)
        got = dot(top, oht_ref[...]) + (dot(middle, oht_ref[...]) + dot(low, oht_ref[...]))
        for cq in range(12):
            rows = pl.ds(a * 12 + cq, 16, stride=WT)
            tall[rows, :] = got[cq * 16 : cq * 16 + 16, :128]
            edge[rows, :] = got[cq * 16 : cq * 16 + 16, 128:]
    split_rows = (kind[0] % 2).astype(F32)
    split_cols = (kind[0] // 2).astype(F32)
    closed = rdiff[...] * split_rows + cdiff[...] * split_cols > 0.0
    for h in range(HEADS):
        rows = slice(h * WT, h * WT + WT)
        out_ref[rows, :128] = jnp.where(closed[:, :128], MASKED, tall[rows, :])
        out_ref[rows, 128:] = jnp.where(closed[:, 128:], MASKED, edge[rows, : WT - 128])

    @pl.when(who[0] == 1)
    def _():
        load_groups(x_ref, xs)
        extract(xs[...].astype(BF), pick_ref, (c0, c1, c2, c3))


def lane_masks():
    lane = lax.broadcasted_iota(jnp.int32, (1, 128), 1)
    return (lane < 64), (lane >= 64)


def stacked(block, scale):
    low, high = lane_masks()
    one = jnp.asarray(scale, F32)
    zero = jnp.zeros((), F32)
    wide = block.astype(F32)
    return jnp.concatenate([jnp.where(low, wide * one, zero), jnp.where(high, wide * one, zero)], axis=0).astype(BF)


def norm_rows(xs, nc_ref, at, count):
    x = xs[at : at + count, :]
    mean = jnp.mean(x, axis=-1, keepdims=True)
    centered = x - mean
    var = jnp.mean(centered * centered, axis=-1, keepdims=True)
    nc_ref[at : at + count, :D] = (centered * lax.rsqrt(var + NORM_EPS)).astype(BF)


def chances_of(proj_ref, bias_ref, w, p):
    lanes = pl.ds(pl.multiple_of(p * 128, 128), 128)
    klanes = pl.ds(pl.multiple_of(D + p * 128, 128), 128)
    rows = slice(w * WT, w * WT + WT)
    qs = stacked(proj_ref[rows, lanes], 0.125)
    k = proj_ref[rows, klanes]
    s = dot_nt(qs, k) + bias_ref[pl.ds(pl.multiple_of(p * TOK, 8), TOK), :]
    peak = jnp.max(s, axis=-1, keepdims=True)
    e = jnp.exp(s - peak)
    chances = e * (1.0 / jnp.sum(e, axis=-1, keepdims=True))
    return qs, k, chances


def forward_core(xs, win, wout, bias_ref, nc_ref, proj_ref, out):
    for at in range(0, TOK, 48):
        norm_rows(xs, nc_ref, at, 48)
    for c in range(0, 3 * D, 512):
        proj_ref[:, c : c + 512] = dot(nc_ref[:, :D], win[:, c : c + 512]).astype(BF)

    @pl.loop(0, PAIRS)
    def _(p):
        vlanes = pl.ds(pl.multiple_of(2 * D + p * 128, 128), 128)
        for w in range(MICRO):
            rows = slice(w * WT, w * WT + WT)
            _, _, chances = chances_of(proj_ref, bias_ref, w, p)
            ch = chances.astype(BF)
            vs = stacked(proj_ref[rows, vlanes], 1.0)
            ctx = dot(ch[:WT], vs[:WT]) + dot(ch[WT:], vs[WT:])
            nc_ref[rows, pl.ds(pl.multiple_of(D + p * 128, 128), 128)] = ctx.astype(BF)

    for c in range(0, D, 512):
        out[:, c : c + 512] = xs[:, c : c + 512] + dot(nc_ref[:, D:], wout[:, c : c + 512])


def backward_core(who, xs, go, win, wout, bias_ref, nc_ref, proj_ref, oh_ref, late, gctx, gp, bacc, edge, fold, out):
    gctx[...] = dot_nt(go[...], wout[...]).astype(BF)
    edge[...] = jnp.zeros_like(edge)

    @pl.loop(0, PAIRS)
    def _(p):
        lanes = pl.ds(pl.multiple_of(p * 128, 128), 128)
        klanes = pl.ds(pl.multiple_of(D + p * 128, 128), 128)
        vlanes = pl.ds(pl.multiple_of(2 * D + p * 128, 128), 128)
        total = None
        for w in range(MICRO):
            rows = slice(w * WT, w * WT + WT)
            qs, k, chances = chances_of(proj_ref, bias_ref, w, p)
            dcs = stacked(gctx[rows, lanes], 1.0)
            dp = dot_nt(dcs, proj_ref[rows, vlanes])
            centre = jnp.sum(dp * chances, axis=-1, keepdims=True)
            ds = chances * (dp - centre)
            total = ds if total is None else total + ds
            dsb = ds.astype(BF)
            gp[rows, vlanes] = dot_tn(chances.astype(BF), dcs).astype(BF)
            gp[rows, klanes] = dot_tn(dsb, qs).astype(BF)
            ks = stacked(k, 0.125)
            gp[rows, lanes] = (dot(dsb[:WT], ks[:WT]) + dot(dsb[WT:], ks[WT:])).astype(BF)
        both = pl.ds(pl.multiple_of(p * TOK, 8), TOK)
        bacc[both, :] = total[:, :128]
        edge[both, : WT - 128] = total[:, 128:]

    for at in range(0, TOK, 96):
        rows = slice(at, at + 96)
        dn = dot_nt(gp[rows, :], win[...]).astype(BF).astype(F32)
        x = xs[rows, :]
        mean = jnp.mean(x, axis=-1, keepdims=True)
        centered = x - mean
        var = jnp.mean(centered * centered, axis=-1, keepdims=True)
        scale = lax.rsqrt(var + NORM_EPS)
        n = centered * scale
        along = jnp.mean(dn * n, axis=-1, keepdims=True)
        level = jnp.mean(dn, axis=-1, keepdims=True)
        dx = (scale * (dn - level - n * along)).astype(BF).astype(F32)
        out[rows, :] = go[rows, :].astype(F32) + dx

    fold[...] = jnp.zeros_like(fold)
    total = jnp.zeros((BIAS_ROWS, OPAD), F32)
    for a in range(12):
        part = jnp.zeros((BIAS_ROWS, OPAD), F32)
        taken = [pl.ds(a * 12 + cq, 16, stride=WT) for cq in range(12)]
        x = jnp.concatenate(
            [jnp.concatenate([ref[rows, :] for rows in taken], axis=0) for ref in (bacc, edge)], axis=1
        )
        top = x.astype(BF)
        low = (x - top.astype(F32)).astype(BF)
        u = dot(top, oh_ref[...]) + dot(low, oh_ref[...])
        u = jnp.concatenate([u, jnp.zeros((192, OPAD - REACH), F32)], axis=1)
        for cq in range(12):
            one = u[cq * 16 : cq * 16 + 16, :]
            part = part + (one if cq == 0 else pltpu.roll(one, cq, 1))
        total = total + (part if SHIFTS[a] == 0 else pltpu.roll(part, SHIFTS[a], 1))
    fold[:, :OPAD] = total

    for d in range(GROUP):
        j = lax.rem(who[1] + d, GROUP)
        late[d][:TOK, :OPAD] = gp[:, pl.ds(pl.multiple_of(j * 768, 128), 768)]
        late[d][:TOK, OPAD:] = go[:, pl.ds(pl.multiple_of(j * 256, 128), 256)]
        slab = fold[:, pl.ds(pl.multiple_of(j * 256, 128), 256)]
        top = slab.astype(BF)
        late[d][TOK:, :256] = top
        late[d][TOK:, 256:512] = (slab - top.astype(F32)).astype(BF)
        late[d][TOK:, 512:] = jnp.zeros((BIAS_ROWS, 512), BF)


def first_forward_body(who, x_ref, win, wout, bias_ref, pick_ref, nc_ref, proj_ref, p0, p1, p2, p3, xs, out):
    @pl.when(who[0] == 0)
    def _():
        load_groups(x_ref, xs)
        forward_core(xs, win, wout, bias_ref, nc_ref, proj_ref, out)
        extract(out[...].astype(BF), pick_ref, (p0, p1, p2, p3))


def second_body(who, r0, r1, r2, r3, c0, c1, c2, c3, win, wout, bias_ref, pick_ref, pickt_ref, oh_ref,
                nc_ref, s0, s1, s2, s3, g0, g1, g2, g3, l0, l1, l2, l3,
                xs, out, go, proj, gctx, gp, bacc, edge, fold):
    @pl.when(who[0] == 1)
    def _():
        xs[...] = insert((r0, r1, r2, r3), pickt_ref)
        go[...] = insert((c0, c1, c2, c3), pickt_ref).astype(BF)
        forward_core(xs, win, wout, bias_ref, nc_ref, proj, out)
        extract(out[...].astype(BF), pick_ref, (s0, s1, s2, s3))
        backward_core(who, xs, go, win, wout, bias_ref, nc_ref, proj, oh_ref, (l0, l1, l2, l3), gctx, gp, bacc, edge, fold, out)
        extract(out[...].astype(BF), pick_ref, (g0, g1, g2, g3))


def first_backward_body(who, x_ref, g0, g1, g2, g3, nc_ref, proj_ref, win, wout, bias_ref, pickt_ref, oh_ref,
                        out_ref, l0, l1, l2, l3, xs, out, go, gctx, gp, bacc, edge, fold):
    @pl.when(who[0] == 0)
    def _():
        load_groups(x_ref, xs)
        go[...] = insert((g0, g1, g2, g3), pickt_ref).astype(BF)
        backward_core(who, xs, go, win, wout, bias_ref, nc_ref, proj_ref, oh_ref, (l0, l1, l2, l3), gctx, gp, bacc, edge, fold, out)
        store_groups(out, out_ref)


def result_body(who, grad_ref, s0, s1, s2, s3, pickt_ref, out_ref, xs):
    @pl.when(who[0] == 0)
    def _():
        out_ref[...] = grad_ref[...]

    @pl.when(who[0] == 1)
    def _():
        xs[...] = insert((s0, s1, s2, s3), pickt_ref)
        store_groups(xs, out_ref)


def weight_body(who, *refs):
    early_a, early_b, late_a, late_b = (refs[4 * i : 4 * i + 4] for i in range(4))
    out_ref, held, grads, terms, sem = refs[16:]

    def copies(early, late):
        made = []
        for d in range(GROUP):
            rows = pl.ds(TOK * d, TOK)
            made.append(pltpu.make_async_copy(early[d], held.at[rows], sem.at[d, 0]))
            made.append(pltpu.make_async_copy(late[d].at[pl.ds(0, TOK)], grads.at[rows], sem.at[d, 1]))
            made.append(pltpu.make_async_copy(late[d].at[pl.ds(TOK, BIAS_ROWS)], terms.at[d], sem.at[d, 2]))
        return made

    @pl.when(who[0] == 0)
    def _():
        for one in copies(early_a, late_a):
            one.start()

    @pl.when(who[0] == 1)
    def _():
        for one in copies(early_b, late_b):
            one.start()

    for one in copies(early_a, late_a):
        one.wait()

    @pl.loop(0, 4)
    def _(rb):
        dst = pl.ds(pl.multiple_of(rb * 16, 16), 16)
        into = dot_tn(held[:, pl.ds(pl.multiple_of(rb * 256, 128), 256)], grads[:, :768])
        for cb in range(6):
            out_ref[dst, cb * 16 : cb * 16 + 16, :] = into[:, cb * 128 : cb * 128 + 128].astype(BF).reshape(16, 16, 128)
        outof = dot_tn(held[:, pl.ds(pl.multiple_of(D + rb * 256, 128), 256)], grads[:, 768:])
        for cb in range(2):
            out_ref[dst, 96 + cb * 16 : 112 + cb * 16, :] = outof[:, cb * 128 : cb * 128 + 128].astype(BF).reshape(16, 16, 128)

    slab = jnp.zeros((BIAS_ROWS, 256), F32)
    for d in range(GROUP):
        slab = slab + (terms[d, :, :256].astype(F32) + terms[d, :, 256:512].astype(F32))
    for half in range(2):
        piece = slab[:, half * 128 : half * 128 + 128].astype(BF)
        out_ref[:, 128 + half * 16 : 144 + half * 16, :] = jnp.broadcast_to(piece[None], (64, BIAS_ROWS, 128))


def sum_body(in_ref, w_ref, b_ref, bias):
    for z in range(GROUP):
        total = None
        for outer in range(8):
            for lon in range(2):
                one = in_ref[(outer * 4 + z) * 2 + lon].astype(F32)
                total = one if total is None else total + one
        for cb in range(6):
            w_ref[:, z * 768 + cb * 128 : z * 768 + cb * 128 + 128] = total[cb * 16 : cb * 16 + 16]
        for cb in range(2):
            at = 3 * D + z * 256 + cb * 128
            w_ref[:, at : at + 128] = total[96 + cb * 16 : 112 + cb * 16]
            bias[:, z * 256 + cb * 128 : z * 256 + cb * 128 + 128] = total[128 + cb * 16 : 144 + cb * 16]
    b_ref[...] = bias[:, :OFFSETS]


def per_device(boundary, tile_kinds, proj_in, proj_out, offset_bias):
    axes = ("lat", "lon", "section")
    nlat, nlon = lax.axis_size("lat"), lax.axis_size("lon")
    section = lax.axis_index("section")
    depth = lax.axis_index("lat") % GROUP
    who = jnp.stack([section, depth]).astype(jnp.int32)
    kind = tile_kinds.reshape(1)
    x = boundary.reshape(TOK // 12, 12, D)
    win = proj_in[0]
    wout = proj_out[0]
    onehot = jnp.asarray(ONEHOT, BF)
    onehot_t = jnp.asarray(ONEHOT.T, BF)
    pick = jnp.asarray(PICK, BF)
    pick_t = jnp.asarray(PICK.transpose(0, 2, 1), BF)

    def flat(lat, lon, sec):
        return ((lat % nlat) * nlon + lon % nlon) * 2 + sec

    def roll_pairs(dl, dn, from_section, to_section):
        return [
            (flat(i, j, from_section), flat(i + dl, j + dn, to_section))
            for i in range(nlat)
            for j in range(nlon)
        ]

    def ring_pairs(step, sections):
        return [
            (flat(i, j, s), flat(i - i % GROUP + (i + step) % GROUP, j, s))
            for i in range(nlat)
            for j in range(nlon)
            for s in sections
        ]

    def forth(pieces, src, dst):
        got = []
        for dl in range(2):
            for dn in range(2):
                piece = pieces[(1 - dl) * 2 + (1 - dn)]
                if src == dst and dl == 0 and dn == 0:
                    got.append(piece)
                else:
                    got.append(lax.ppermute(piece, axes, roll_pairs(-dl, -dn, src, dst)))
        return got

    def back(pieces, src, dst):
        got = [None] * 4
        for dl in range(2):
            for dn in range(2):
                piece = pieces[dl * 2 + dn]
                if not (src == dst and dl == 0 and dn == 0):
                    piece = lax.ppermute(piece, axes, roll_pairs(dl, dn, src, dst))
                got[(1 - dl) * 2 + (1 - dn)] = piece
        return got

    def round_ring(values, sections):
        return [values[0]] + [
            lax.ppermute(values[d], axes, ring_pairs(d, sections)) for d in range(1, GROUP)
        ]

    quarter = [shape(QT, D)] * 4
    late = [shape(TOK + BIAS_ROWS, D)] * 4
    f32 = functools.partial(shape, dtype=F32)
    vf32 = lambda *dims: pltpu.VMEM(dims, F32)
    vbf = lambda *dims: pltpu.VMEM(dims, BF)

    bias, *cots = call(
        bias_body, "bias_table", [f32(HEADS * WT, WT)] + quarter,
        [SMEM, SMEM] + [VMEM] * 6,
        [vf32(TOK, D), vf32(HEADS, OPAD), vf32(12 * 192, REACH), vf32(HEADS * WT, 128), vf32(HEADS * WT, 128)], 2_000_000_000, 4_000_000,
    )(who, kind, x, offset_bias[0], onehot_t, jnp.asarray(ROWS_DIFFER), jnp.asarray(COLS_DIFFER), pick)
    cots = forth(cots, 1, 1)

    nc_a, proj_a, *pieces = call(
        first_forward_body, "first_forward", [shape(TOK, 2 * D), shape(TOK, 3 * D)] + quarter,
        [SMEM] + [VMEM] * 5,
        [vf32(TOK, D), vf32(TOK, D)], 3_000_000_000, 20_000_000,
    )(who, x, win, wout, bias, pick)
    received = forth(pieces, 0, 1)
    received, nc_a = lax.optimization_barrier((received, nc_a))
    early_a = round_ring([nc_a] * 4, (0,))

    back_scratch = [vbf(TOK, D), vbf(TOK, 3 * D), vf32(HEADS * WT, 128), vf32(HEADS * WT, 128), vf32(BIAS_ROWS, D)]
    nc_b, *more = call(
        second_body, "second_both", [shape(TOK, 2 * D)] + quarter * 2 + late,
        [SMEM] + [VMEM] * 14,
        [vf32(TOK, D), vf32(TOK, D), vbf(TOK, D), vbf(TOK, 3 * D)] + back_scratch, 9_000_000_000, 20_000_000,
    )(who, *received, *cots, win, wout, bias, pick, pick_t, onehot)
    second_out, grads, late_b = more[:4], more[4:8], more[8:]
    grads = back(grads, 1, 0)
    grads, second_out, late_b, nc_b = lax.optimization_barrier((grads, second_out, late_b, nc_b))
    late_b = round_ring(late_b, (1,))
    early_b = round_ring([nc_b] * 4, (1,))
    second_out = back(second_out, 1, 1)

    grad_in, *late_a = call(
        first_backward_body, "first_backward", [shape(TOK // 12, 12, D)] + late,
        [SMEM] + [VMEM] * 12,
        [vf32(TOK, D), vf32(TOK, D), vbf(TOK, D)] + back_scratch, 6_000_000_000, 20_000_000,
    )(who, x, *grads, nc_a, proj_a, win, wout, bias, pick_t, onehot)
    late_a = round_ring(late_a, (0,))

    result = call(
        result_body, "result", shape(TOK // 12, 12, D), [SMEM] + [VMEM] * 6, [vf32(TOK, D)], 170_000_000, 2_000_000,
    )(who, grad_in, *second_out, pick_t)

    terms = call(
        weight_body, "weight_terms", shape(64, 160, 128), [SMEM] + [ANY] * 16,
        [vbf(GROUP * TOK, 2 * D), vbf(GROUP * TOK, D), vbf(GROUP, BIAS_ROWS, D), pltpu.SemaphoreType.DMA((GROUP, 3))],
        2_400_000_000, 10_000_000,
    )(who, *early_a, *early_b, *late_a, *late_b)
    terms = lax.all_to_all(terms, ("lat", "lon"), 0, 0, tiled=True)

    weights, table = call(
        sum_body, "sum_terms", [f32(16, 4 * D), f32(HEADS, OFFSETS)], [VMEM], [vf32(HEADS, D)], 3_000_000, 3_000_000,
    )(terms)
    return (result.reshape(boundary.shape), weights[None], table[None])


def solution(mesh):
    return jax.shard_map(
        per_device,
        mesh=mesh,
        in_specs=(
            P("section", None, None, "lat", "lon", None),
            P("section", "lat", "lon"),
            P("section", None, None),
            P("section", None, None),
            P("section", None, None),
        ),
        out_specs=(
            P("section", None, None, "lat", "lon", None),
            P("section", ("lat", "lon"), None),
            P("section", None, None),
        ),
        check_vma=False,
    )
```

time: 953 us -> 247 us (0.26); the launches traced: 941 us -> 246 us
  blocking collectives: 353 us -> 0 us
  local copies, waits for them, and re-layouts: 219 us -> 10.5 us
  matrix products: 168 us -> 0 us
  Pallas kernels: 0 us -> 73.6 us
  other arithmetic: 60.4 us -> 0.65 us
  starting transfers between devices: 28 us -> 46.9 us
  waiting for transfers between devices: 95.8 us -> 113 us
  between operations: 16.2 us -> 1.97 us
    psum x1 -> x0, blocking collectives: 353 us -> none  [per_device(): bias_sum = lax.psum(bias_total, ('lat', 'lon'))]
    dot_general x28 -> x0, matrix products: 168 us -> none  [the longest x2 62.1 us: pair_bias(): jnp.einsum('hxabcd,efx->heacfbd', along_rows, offset_table(LEV), precisio...]
    pallas_call x0 -> x7, Pallas kernels: none -> 73.6 us  [the longest x1 28.3 us: per_device(): call(first_backward_body, 'first_backward', [shape(TOK // 12, 12, D)] + l...]
    add x5 -> x0, local copies, waits for them, and re-layouts: 56.4 us -> none  [the longest x2 39.7 us: attend(): scores = jnp.where(allowed[:, None], scores + bias_full[None], MASKED)]
    transpose x3 -> x0, local copies, waits for them, and re-layouts: 26.4 us -> none  [the longest x1 20.7 us: pair_bias(): jnp.einsum('hxycd,aby->hxabcd', along_cols, offset_table(WIN_LAT), precis...]
    select_n x10 -> x0, local copies, waits for them, and re-layouts: 24.8 us -> none  [the longest x6 21.6 us: per_device(): jnp.where(is_first, left_part, right_part)]
    reshape x8 -> x0, local copies, waits for them, and re-layouts: 21 us -> none  [the longest x2 11.5 us: backward(): from_windows(grad_windows, moved.shape[:4]).reshape(-1, 3 * features)]
    unnamed x133 -> x78, local copies, waits for them, and re-layouts: 29.2 us -> 10.5 us
  transfers between devices with their start and end apart: 19 -> 27, of which waited for: 11 -> 8; matrix products, arithmetic and copies ran while one was open for 28% -> 1% of each run, Pallas kernels for 0% -> 1%
where the time goes in v1:
time: 247 us; the launch traced here: 246 us
  waiting for transfers between devices  113 us (46%)
  Pallas kernels  73.6 us (30%)
  starting transfers between devices  46.9 us (19%)
  local copies, waits for them, and re-layouts  10.5 us (4%)
    ppermute x7, waiting for transfers between devices, back(): piece = lax.ppermute(piece, axes, roll_pairs(dl, dn, src, dst))  50 us
    ppermute x12, waiting for transfers between devices, round_ring(): lax.ppermute(values[d], axes, ring_pairs(d, sections))  45.7 us
    pallas_call x1, Pallas kernels, per_device(): call(first_backward_body, 'first_backward', [shape(TOK // 12, 12, D)] + l...  28.3 us
    ppermute x12, starting transfers between devices, round_ring(): lax.ppermute(values[d], axes, ring_pairs(d, sections))  23.3 us
    pallas_call x1, Pallas kernels, per_device(): call(first_forward_body, 'first_forward', [shape(TOK, 2 * D), shape(TOK,...  18 us
    all_to_all x1, waiting for transfers between devices, per_device(): terms = lax.all_to_all(terms, ('lat', 'lon'), 0, 0, tiled=True)  14.7 us
    unnamed x78, local copies, waits for them, and re-layouts  10.5 us
    all_to_all x1, starting transfers between devices, per_device(): terms = lax.all_to_all(terms, ('lat', 'lon'), 0, 0, tiled=True)  9 us
  transfers between devices with their start and end apart: 27, of which 8 were waited for; matrix products, arithmetic and copies ran while one was open for 1% of the time, Pallas kernels for 1%

profile of v1, /device:TPU:0, one launch (start us, length us, event | category | flops | bytes accessed | tf_op | source)
XLA Modules:
  0.0 246.3 jit_solution(11516875325205161950)
XLA Ops:
  0.6 2.1 copy.14
  4.1 6.1 %bias_table.1 = (f32[2304,144]{1,0:T(8,128)}, bf16[72,1024]{1,0:T(8,128)(2,1)}, bf16[72,1024]{1,0:T(8,128)(2,1)}, bf16[72,1024]{1,0:T(8,128)(2,1)}, bf16[72,1024]{1,0:T(8,128)(2,1)}) custom-call(s32[2]{0:T(128)} %pad_add_fusion.who, s32[1]{0:T(128)} %bitcast.10.kind, bf16[24,12,1024]{2,1,0:T(8,128)(2,1)} %bitcast.14, f32[16,759]{1,0:T(8,128)} %bitcast.22, ...), custom_call_target="tpu_custom_call" | custom-call | flops 2000000000 | bytes 4000000 | tf_op jit(solution)/shard_map/bias_table/pallas_call | solution.py:441
  10.2 18.0 %first_forward.1 = (bf16[288,2048]{1,0:T(8,128)(2,1)}, bf16[288,3072]{1,0:T(8,128)(2,1)}, bf16[72,1024]{1,0:T(8,128)(2,1)}, bf16[72,1024]{1,0:T(8,128)(2,1)}, bf...) custom-call(s32[2]{0:T(128)} %pad_add_fusion.who, bf16[24,12,1024]{2,1,0:T(8,128)(2,1)} %bitcast.15, ...), custom_call_target="tpu_custom_call" | custom-call | flops 3000000000 | bytes 20000000 | tf_op jit(solution)/shard_map/first_forward/pallas_call | solution.py:448
  35.5 2.4 collective-permute-done.3.r3
  38.7 7.1 %second_both.1 = (bf16[288,2048]{1,0:T(8,128)(2,1)}, bf16[72,1024]{1,0:T(8,128)(2,1)}, bf16[72,1024]{1,0:T(8,128)(2,1)}, bf16[72,1024]{1,0:T(8,128)(2,1)}, bf16[...) custom-call(s32[2]{0:T(128)} %pad_add_fusion.who, ...), custom_call_target="tpu_custom_call" | custom-call | flops 8999999488 | bytes 20000000 | tf_op jit(solution)/shard_map/second_both/pallas_call | solution.py:458
  49.8 1.5 collective-permute-start.10
  51.3 49.9 %collective-permute-done.7.g0 = bf16[72,1024]{1,0:T(8,128)(2,1)S(1)} collective-permute-done((bf16[72,1024]{1,0:T(8,128)(2,1)}, bf16[72,1024]{1,0:T(8,128)(2,1)S(1)}, u32[]{:S(2)}, u32[]{:S(2)}) %collective-permute-start.7) | collective-permute-done | bytes 147488 | tf_op jit(solution)/shard_map/ppermute | solution.py:426
  102.1 28.3 %first_backward.1 = (bf16[24,12,1024]{2,1,0:T(8,128)(2,1)}, bf16[304,1024]{1,0:T(8,128)(2,1)}, bf16[304,1024]{1,0:T(8,128)(2,1)}, bf16[304,1024]{1,0:T(8,128)(2,1)}, bf16[304,1024]{1,0:T(8,128)(2,1)}) custom-call(s32[2]{0:T(128)} %pad_add_fusion.who, bf16[24,12,1024]{2,1,0:T(8,128)(2,1)} %bitcast.16, bf16[72,1024]{1,0:T(8,128)(2,1)} %copy-done.34, ...), custom_call_target="tpu_custom_call" | custom-call | flops 6000000000 | bytes 20000000 | tf_op jit(solution)/shard_map/first_backward/pallas_call | solution.py:470
  130.3 1.9 collective-permute-start.20
  132.2 1.9 collective-permute-start.21
  134.2 6.0 %collective-permute-start.14 = (bf16[288,2048]{1,0:T(8,128)(2,1)S(1)}, bf16[288,2048]{1,0:T(8,128)(2,1)S(1)}, u32[]{:S(2)}, u32[]{:S(2)}) collective-permute-start(bf16[288,2048]{1,0:T(8,128)(2,1)S(1)} %copy-done.1), channel_id=1, source_target_pairs={{0,4},{2,6},{4,8},{6,10},{8,12},{10,14},{12,0},{14,2},{16,20},{18,... | collective-permute-start | bytes 3538952 | tf_op jit(solution)/shard_map/ppermute | solution.py:432
  140.2 1.9 collective-permute-start.22
  142.8 16.4 %collective-permute-done.20.refs_9_ = bf16[304,1024]{1,0:T(8,128)(2,1)S(1)} collective-permute-done((bf16[304,1024]{1,0:T(8,128)(2,1)}, bf16[304,1024]{1,0:T(8,128)(2,1)S(1)}, u32[]{:S(2)}, u32[]{:S(2)}) %collective-permute-start.20) | collective-permute-done | bytes 622624 | tf_op jit(solution)/shard_map/ppermute | solution.py:432
  161.1 5.6 %collective-permute-done.22.refs_11_ = bf16[304,1024]{1,0:T(8,128)(2,1)S(1)} collective-permute-done((bf16[304,1024]{1,0:T(8,128)(2,1)}, bf16[304,1024]{1,0:T(8,128)(2,1)S(1)}, u32[]{:S(2)}, u32[]{:S(2)}) %collective-permute-start.22) | collective-permute-done | bytes 622624 | tf_op jit(solution)/shard_map/ppermute | solution.py:432
  166.7 2.5 %collective-permute-start.15 = (bf16[288,2048]{1,0:T(8,128)(2,1)S(1)}, bf16[288,2048]{1,0:T(8,128)(2,1)S(1)}, u32[]{:S(2)}, u32[]{:S(2)}) collective-permute-start(bf16[288,2048]{1,0:T(8,128)(2,1)S(1)} %copy-done.1), channel_id=1, source_target_pairs={{0,8},{2,10},{4,12},{6,14},{8,0},{10,2},{12,4},{14,6},{16,24},{18,... | collective-permute-start | bytes 3538952 | tf_op jit(solution)/shard_map/ppermute | solution.py:432
  169.3 4.8 %collective-permute-start.16 = (bf16[288,2048]{1,0:T(8,128)(2,1)S(1)}, bf16[288,2048]{1,0:T(8,128)(2,1)S(1)}, u32[]{:S(2)}, u32[]{:S(2)}) collective-permute-start(bf16[288,2048]{1,0:T(8,128)(2,1)S(1)} %copy-done.1), channel_id=1, source_target_pairs={{0,12},{2,14},{4,0},{6,2},{8,4},{10,6},{12,8},{14,10},{16,28},{18,... | collective-permute-start | bytes 3538952 | tf_op jit(solution)/shard_map/ppermute | solution.py:432
  175.6 20.3 %collective-permute-done.14.refs_1_ = bf16[288,2048]{1,0:T(8,128)(2,1)S(1)} collective-permute-done((bf16[288,2048]{1,0:T(8,128)(2,1)S(1)}, bf16[288,2048]{1,0:T(8,128)(2,1)S(1)}, u32[]{:S(2)}, u32[]{:S(2)}) %collective-permute-start.14) | collective-permute-done | bytes 1179680 | tf_op jit(solution)/shard_map/ppermute | solution.py:432
  196.6 2.9 %collective-permute-done.16.refs_3_ = bf16[288,2048]{1,0:T(8,128)(2,1)S(1)} collective-permute-done((bf16[288,2048]{1,0:T(8,128)(2,1)S(1)}, bf16[288,2048]{1,0:T(8,128)(2,1)S(1)}, u32[]{:S(2)}, u32[]{:S(2)}) %collective-permute-start.16) | collective-permute-done | bytes 1179680 | tf_op jit(solution)/shard_map/ppermute | solution.py:432
  201.6 8.9 %weight_terms.1 = bf16[64,160,128]{2,1,0:T(8,128)(2,1)} custom-call(s32[2]{0:T(128)} %pad_add_fusion.who, bf16[288,2048]{1,0:T(8,128)(2,1)} %get-tuple-element.83.nc_ref.refs_0_, bf16[288,2048]{1,0:T(8,128)(2,1)} %copy-done.3, bf16[288,2048]{1,0:T(8,128)(2,1)} %copy-done.4, bf16[288,2048]{1,0:T(8,128)(2,1)} %copy-done.5, ...), custom_call_target="tpu_custom_call" | custom-call | flops 2400000000 | bytes 10000000 | tf_op jit(solution)/shard_map/weight_terms/pallas_call | solution.py:481
  210.6 9.0 %all-to-all-start = ((bf16[64,160,128]{2,1,0:T(8,128)(2,1)}), bf16[64,160,128]{2,1,0:T(8,128)(2,1)S(1)}, u32[]{:S(2)}, u32[]{:S(2)}) async-start(bf16[64,160,128]{2,1,0:T(8,128)(2,1)} %weight_terms.1), calls=%async_computation | async-start | bytes 5242880 | tf_op jit(solution)/shard_map/all_to_all | solution.py:486
  222.4 2.4 result.1
  224.8 2.6 %copy.15 = bf16[1,2,2,6,12,1024]{5,2,4,3,1,0:T(2,128)(2,1)} copy(bf16[1,2,2,6,12,1024]{5,4,3,2,1,0:T(8,128)(2,1)} %bitcast.17) | data formatting | bytes 1179648
  227.4 14.7 %all-to-all-done.in_ref = bf16[64,160,128]{2,1,0:T(8,128)(2,1)S(1)} async-done(((bf16[64,160,128]{2,1,0:T(8,128)(2,1)}), bf16[64,160,128]{2,1,0:T(8,128)(2,1)S(1)}, u32[]{:S(2)}, u32[]{:S(2)}) %all-to-all-start) | async-done | bytes 2621472 | tf_op jit(solution)/shard_map/all_to_all | solution.py:486
  243.6 2.7 %sum_terms.1 = (f32[16,4096]{1,0:T(8,128)}, f32[16,759]{1,0:T(8,128)}) custom-call(bf16[64,160,128]{2,1,0:T(8,128)(2,1)} %copy-done), custom_call_target="tpu_custom_call" | custom-call | flops 3000000 | bytes 3000000 | tf_op jit(solution)/shard_map/sum_terms/pallas_call | solution.py:488
  (116 shorter events, 24.4 us)
Async XLA Ops:
  28.2 5.9 %collective-permute-start = (bf16[72,1024]{1,0:T(8,128)(2,1)}, bf16[72,1024]{1,0:T(8,128)(2,1)S(1)}, u32[]{:S(2)}, u32[]{:S(2)}) collective-permute-start(bf16[72,1024]{1,0:T(8,128)(2,1)} %get-tuple-element.53), channel_id=1, source_target_pairs={{0,1},{2,3},{4,5},{6,7},{8,9},{10,11},{12,13},{14,15},{16,17},{18,... | collective-permute-start | bytes 442376 | tf_op jit(solution)/shard_map/ppermute | solution.py:417
  29.5 5.3 %collective-permute-start.1 = (bf16[72,1024]{1,0:T(8,128)(2,1)}, bf16[72,1024]{1,0:T(8,128)(2,1)S(1)}, u32[]{:S(2)}, u32[]{:S(2)}) collective-permute-start(bf16[72,1024]{1,0:T(8,128)(2,1)} %get-tuple-element.54), channel_id=1, source_target_pairs={{0,3},{2,1},{4,7},{6,5},{8,11},{10,9},{12,15},{14,13},{16,19},{18,... | collective-permute-start | bytes 442376 | tf_op jit(solution)/shard_map/ppermute | solution.py:417
  30.8 4.7 %collective-permute-start.2 = (bf16[72,1024]{1,0:T(8,128)(2,1)}, bf16[72,1024]{1,0:T(8,128)(2,1)S(1)}, u32[]{:S(2)}, u32[]{:S(2)}) collective-permute-start(bf16[72,1024]{1,0:T(8,128)(2,1)} %get-tuple-element.55), channel_id=1, source_target_pairs={{0,125},{2,127},{4,1},{6,3},{8,5},{10,7},{12,9},{14,11},{16,13},{1... | collective-permute-start | bytes 442376 | tf_op jit(solution)/shard_map/ppermute | solution.py:417
  32.1 5.8 %collective-permute-start.3 = (bf16[72,1024]{1,0:T(8,128)(2,1)}, bf16[72,1024]{1,0:T(8,128)(2,1)S(1)}, u32[]{:S(2)}, u32[]{:S(2)}) collective-permute-start(bf16[72,1024]{1,0:T(8,128)(2,1)} %get-tuple-element.56), channel_id=1, source_target_pairs={{0,127},{2,125},{4,3},{6,1},{8,7},{10,5},{12,11},{14,9},{16,15},{1... | collective-permute-start | bytes 442376 | tf_op jit(solution)/shard_map/ppermute | solution.py:417
  33.4 4.5 %collective-permute-start.4 = (bf16[72,1024]{1,0:T(8,128)(2,1)S(1)}, bf16[72,1024]{1,0:T(8,128)(2,1)S(1)}, u32[]{:S(2)}, u32[]{:S(2)}) collective-permute-start(bf16[72,1024]{1,0:T(8,128)(2,1)S(1)} %copy-done.29), channel_id=1, source_target_pairs={{1,3},{3,1},{5,7},{7,5},{9,11},{11,9},{13,15},{15,13},{17,19},{19,... | collective-permute-start | bytes 442376 | tf_op jit(solution)/shard_map/ppermute | solution.py:417
  34.1 3.8 %collective-permute-start.5 = (bf16[72,1024]{1,0:T(8,128)(2,1)S(1)}, bf16[72,1024]{1,0:T(8,128)(2,1)S(1)}, u32[]{:S(2)}, u32[]{:S(2)}) collective-permute-start(bf16[72,1024]{1,0:T(8,128)(2,1)S(1)} %copy-done.27), channel_id=1, source_target_pairs={{1,125},{3,127},{5,1},{7,3},{9,5},{11,7},{13,9},{15,11},{17,13},{1... | collective-permute-start | bytes 442376 | tf_op jit(solution)/shard_map/ppermute | solution.py:417
  34.8 3.1 %collective-permute-start.6 = (bf16[72,1024]{1,0:T(8,128)(2,1)S(1)}, bf16[72,1024]{1,0:T(8,128)(2,1)S(1)}, u32[]{:S(2)}, u32[]{:S(2)}) collective-permute-start(bf16[72,1024]{1,0:T(8,128)(2,1)S(1)} %copy-done.25), channel_id=1, source_target_pairs={{1,127},{3,125},{5,3},{7,1},{9,7},{11,5},{13,11},{15,9},{17,15},{1... | collective-permute-start | bytes 442376 | tf_op jit(solution)/shard_map/ppermute | solution.py:417
  45.9 55.4 %collective-permute-start.7 = (bf16[72,1024]{1,0:T(8,128)(2,1)}, bf16[72,1024]{1,0:T(8,128)(2,1)S(1)}, u32[]{:S(2)}, u32[]{:S(2)}) collective-permute-start(bf16[72,1024]{1,0:T(8,128)(2,1)} %get-tuple-element.66), channel_id=1, source_target_pairs={{1,6},{3,4},{5,10},{7,8},{9,14},{11,12},{13,18},{15,16},{17,22},{1... | collective-permute-start | bytes 442376 | tf_op jit(solution)/shard_map/ppermute | solution.py:426
  47.2 54.1 %collective-permute-start.8 = (bf16[72,1024]{1,0:T(8,128)(2,1)}, bf16[72,1024]{1,0:T(8,128)(2,1)S(1)}, u32[]{:S(2)}, u32[]{:S(2)}) collective-permute-start(bf16[72,1024]{1,0:T(8,128)(2,1)} %get-tuple-element.67), channel_id=1, source_target_pairs={{1,4},{3,6},{5,8},{7,10},{9,12},{11,14},{13,16},{15,18},{17,20},{1... | collective-permute-start | bytes 442376 | tf_op jit(solution)/shard_map/ppermute | solution.py:426
  48.5 52.8 %collective-permute-start.9 = (bf16[72,1024]{1,0:T(8,128)(2,1)}, bf16[72,1024]{1,0:T(8,128)(2,1)S(1)}, u32[]{:S(2)}, u32[]{:S(2)}) collective-permute-start(bf16[72,1024]{1,0:T(8,128)(2,1)} %get-tuple-element.68), channel_id=1, source_target_pairs={{1,2},{3,0},{5,6},{7,4},{9,10},{11,8},{13,14},{15,12},{17,18},{19,... | collective-permute-start | bytes 442376 | tf_op jit(solution)/shard_map/ppermute | solution.py:426
  49.8 51.5 %collective-permute-start.10 = (bf16[72,1024]{1,0:T(8,128)(2,1)}, bf16[72,1024]{1,0:T(8,128)(2,1)S(1)}, u32[]{:S(2)}, u32[]{:S(2)}) collective-permute-start(bf16[72,1024]{1,0:T(8,128)(2,1)} %get-tuple-element.69), channel_id=1, source_target_pairs={{1,0},{3,2},{5,4},{7,6},{9,8},{11,10},{13,12},{15,14},{17,16},{19,... | collective-permute-start | bytes 442376 | tf_op jit(solution)/shard_map/ppermute | solution.py:426
  130.3 28.8 %collective-permute-start.20 = (bf16[304,1024]{1,0:T(8,128)(2,1)}, bf16[304,1024]{1,0:T(8,128)(2,1)S(1)}, u32[]{:S(2)}, u32[]{:S(2)}) collective-permute-start(bf16[304,1024]{1,0:T(8,128)(2,1)} %get-tuple-element.92), channel_id=1, source_target_pairs={{0,4},{2,6},{4,8},{6,10},{8,12},{10,14},{12,0},{14,2},{16,20},{18,... | collective-permute-start | bytes 1867784 | tf_op jit(solution)/shard_map/ppermute | solution.py:432
  132.2 28.2 %collective-permute-start.21 = (bf16[304,1024]{1,0:T(8,128)(2,1)}, bf16[304,1024]{1,0:T(8,128)(2,1)S(1)}, u32[]{:S(2)}, u32[]{:S(2)}) collective-permute-start(bf16[304,1024]{1,0:T(8,128)(2,1)} %get-tuple-element.93), channel_id=1, source_target_pairs={{0,8},{2,10},{4,12},{6,14},{8,0},{10,2},{12,4},{14,6},{16,24},{18,... | collective-permute-start | bytes 1867784 | tf_op jit(solution)/shard_map/ppermute | solution.py:432
  134.2 61.7 %collective-permute-start.14 = (bf16[288,2048]{1,0:T(8,128)(2,1)S(1)}, bf16[288,2048]{1,0:T(8,128)(2,1)S(1)}, u32[]{:S(2)}, u32[]{:S(2)}) collective-permute-start(bf16[288,2048]{1,0:T(8,128)(2,1)S(1)} %copy-done.1), channel_id=1, source_target_pairs={{0,4},{2,6},{4,8},{6,10},{8,12},{10,14},{12,0},{14,2},{16,20},{18,... | collective-permute-start | bytes 3538952 | tf_op jit(solution)/shard_map/ppermute | solution.py:432
  140.2 26.5 %collective-permute-start.22 = (bf16[304,1024]{1,0:T(8,128)(2,1)}, bf16[304,1024]{1,0:T(8,128)(2,1)S(1)}, u32[]{:S(2)}, u32[]{:S(2)}) collective-permute-start(bf16[304,1024]{1,0:T(8,128)(2,1)} %get-tuple-element.94), channel_id=1, source_target_pairs={{0,12},{2,14},{4,0},{6,2},{8,4},{10,6},{12,8},{14,10},{16,28},{18,... | collective-permute-start | bytes 1867784 | tf_op jit(solution)/shard_map/ppermute | solution.py:432
  142.1 27.1 %collective-permute-start.23 = (bf16[304,1024]{1,0:T(8,128)(2,1)S(1)}, bf16[304,1024]{1,0:T(8,128)(2,1)S(1)}, u32[]{:S(2)}, u32[]{:S(2)}) collective-permute-start(bf16[304,1024]{1,0:T(8,128)(2,1)S(1)} %copy-done.20), channel_id=1, source_target_pairs={{1,5},{3,7},{5,9},{7,11},{9,13},{11,15},{13,1},{15,3},{17,21},{19,... | collective-permute-start | bytes 1867784 | tf_op jit(solution)/shard_map/ppermute | solution.py:432
  159.2 14.9 %collective-permute-start.24 = (bf16[304,1024]{1,0:T(8,128)(2,1)S(1)}, bf16[304,1024]{1,0:T(8,128)(2,1)S(1)}, u32[]{:S(2)}, u32[]{:S(2)}) collective-permute-start(bf16[304,1024]{1,0:T(8,128)(2,1)S(1)} %copy-done.19), channel_id=1, source_target_pairs={{1,9},{3,11},{5,13},{7,15},{9,1},{11,3},{13,5},{15,7},{17,25},{19,... | collective-permute-start | bytes 1867784 | tf_op jit(solution)/shard_map/ppermute | solution.py:432
  160.4 14.4 %collective-permute-start.25 = (bf16[304,1024]{1,0:T(8,128)(2,1)S(1)}, bf16[304,1024]{1,0:T(8,128)(2,1)S(1)}, u32[]{:S(2)}, u32[]{:S(2)}) collective-permute-start(bf16[304,1024]{1,0:T(8,128)(2,1)S(1)} %copy-done.18), channel_id=1, source_target_pairs={{1,13},{3,15},{5,1},{7,3},{9,5},{11,7},{13,9},{15,11},{17,29},{19,... | collective-permute-start | bytes 1867784 | tf_op jit(solution)/shard_map/ppermute | solution.py:432
  166.7 29.9 %collective-permute-start.15 = (bf16[288,2048]{1,0:T(8,128)(2,1)S(1)}, bf16[288,2048]{1,0:T(8,128)(2,1)S(1)}, u32[]{:S(2)}, u32[]{:S(2)}) collective-permute-start(bf16[288,2048]{1,0:T(8,128)(2,1)S(1)} %copy-done.1), channel_id=1, source_target_pairs={{0,8},{2,10},{4,12},{6,14},{8,0},{10,2},{12,4},{14,6},{16,24},{18,... | collective-permute-start | bytes 3538952 | tf_op jit(solution)/shard_map/ppermute | solution.py:432
  169.3 30.2 %collective-permute-start.16 = (bf16[288,2048]{1,0:T(8,128)(2,1)S(1)}, bf16[288,2048]{1,0:T(8,128)(2,1)S(1)}, u32[]{:S(2)}, u32[]{:S(2)}) collective-permute-start(bf16[288,2048]{1,0:T(8,128)(2,1)S(1)} %copy-done.1), channel_id=1, source_target_pairs={{0,12},{2,14},{4,0},{6,2},{8,4},{10,6},{12,8},{14,10},{16,28},{18,... | collective-permute-start | bytes 3538952 | tf_op jit(solution)/shard_map/ppermute | solution.py:432
  174.1 25.4 %collective-permute-start.17 = (bf16[288,2048]{1,0:T(8,128)(2,1)S(1)}, bf16[288,2048]{1,0:T(8,128)(2,1)S(1)}, u32[]{:S(2)}, u32[]{:S(2)}) collective-permute-start(bf16[288,2048]{1,0:T(8,128)(2,1)S(1)} %copy-done.2), channel_id=1, source_target_pairs={{1,5},{3,7},{5,9},{7,11},{9,13},{11,15},{13,1},{15,3},{17,21},{19,... | collective-permute-start | bytes 3538952 | tf_op jit(solution)/shard_map/ppermute | solution.py:432
  174.8 24.7 %collective-permute-start.18 = (bf16[288,2048]{1,0:T(8,128)(2,1)S(1)}, bf16[288,2048]{1,0:T(8,128)(2,1)S(1)}, u32[]{:S(2)}, u32[]{:S(2)}) collective-permute-start(bf16[288,2048]{1,0:T(8,128)(2,1)S(1)} %copy-done.2), channel_id=1, source_target_pairs={{1,9},{3,11},{5,13},{7,15},{9,1},{11,3},{13,5},{15,7},{17,25},{19,... | collective-permute-start | bytes 3538952 | tf_op jit(solution)/shard_map/ppermute | solution.py:432
  195.9 3.7 %collective-permute-start.19 = (bf16[288,2048]{1,0:T(8,128)(2,1)S(1)}, bf16[288,2048]{1,0:T(8,128)(2,1)S(1)}, u32[]{:S(2)}, u32[]{:S(2)}) collective-permute-start(bf16[288,2048]{1,0:T(8,128)(2,1)S(1)} %copy-done.2), channel_id=1, source_target_pairs={{1,13},{3,15},{5,1},{7,3},{9,5},{11,7},{13,9},{15,11},{17,29},{19,... | collective-permute-start | bytes 3538952 | tf_op jit(solution)/shard_map/ppermute | solution.py:432
  210.6 31.5 %all-to-all-start = ((bf16[64,160,128]{2,1,0:T(8,128)(2,1)}), bf16[64,160,128]{2,1,0:T(8,128)(2,1)S(1)}, u32[]{:S(2)}, u32[]{:S(2)}) async-start(bf16[64,160,128]{2,1,0:T(8,128)(2,1)} %weight_terms.1), calls=%async_computation | async-start | bytes 5242880 | tf_op jit(solution)/shard_map/all_to_all | solution.py:486
  (41 other events, 544.0 us)

commit v2 on v1

v2 whole, which is shorter than its diff:
```python
import functools

import jax
import jax.numpy as jnp
import numpy as np
from jax import lax
from jax.experimental import pallas as pl
from jax.experimental.pallas import tpu as pltpu
from jax.sharding import PartitionSpec as P

D = 1024
HEADS = 16
LEV = 2
MICRO = 2
WIN_LAT = 6
WIN_LON = 12
WT = 144
TOK = MICRO * WT
QT = TOK // 4
OFFSETS = 759
OPAD = 768
LEVEL_STEP = 253
ROW_STEP = 23
PAIRS = HEADS // 2
GROUP = 4
BIAS_ROWS = 16
NORM_EPS = 1e-05
MASKED = -1e30
BF = jnp.bfloat16
F32 = jnp.float32
VLIMIT = 58 * 1024 * 1024
SMALL = 24 * 1024 * 1024

HBM = pl.BlockSpec(memory_space=pltpu.HBM)
VMEM = pl.BlockSpec(memory_space=pltpu.VMEM)
SMEM = pl.BlockSpec(memory_space=pltpu.SMEM)


def constants():
    tok = np.arange(WT)
    lev, row, col = tok // 72, tok // 12 % 6, tok % 12
    onehot = np.zeros((256, 256), np.float32)
    onehot[tok, 128 * lev + 126 - 23 * row - col] = 1
    rows_differ = ((row < 3)[:, None] != (row < 3)[None, :]).astype(np.float32)
    cols_differ = ((col < 6)[:, None] != (col < 6)[None, :]).astype(np.float32)
    pick = np.zeros((4, QT, TOK), np.float32)
    for half_row in range(2):
        for half_col in range(2):
            at = 0
            for micro in range(MICRO):
                for level in range(LEV):
                    for r in range(3):
                        for c in range(6):
                            src = micro * WT + level * 72 + (3 * half_row + r) * 12 + 6 * half_col + c
                            pick[half_row * 2 + half_col, at, src] = 1
                            at += 1
    return onehot, rows_differ, cols_differ, pick


ONEHOT, ROWS_DIFFER, COLS_DIFFER, PICK = constants()


def dot(a, b):
    return jnp.dot(a, b, preferred_element_type=F32)


def dot_nt(a, b):
    return lax.dot_general(a, b, (((1,), (1,)), ((), ())), preferred_element_type=F32)


def dot_tn(a, b):
    return lax.dot_general(a, b, (((0,), (0,)), ((), ())), preferred_element_type=F32)


def call(body, name, out_shape, in_specs, scratch, flops, nbytes, out_specs=None, limit=VLIMIT):
    if out_specs is None:
        out_specs = jax.tree.map(lambda _: VMEM, out_shape)
    return pl.pallas_call(
        body,
        out_shape=out_shape,
        in_specs=in_specs,
        out_specs=out_specs,
        scratch_shapes=scratch,
        compiler_params=pltpu.CompilerParams(vmem_limit_bytes=limit),
        cost_estimate=pl.CostEstimate(flops=flops, bytes_accessed=nbytes, transcendentals=0),
        name=name,
    )


def begin(src, dst, sem):
    copy = pltpu.make_async_copy(src, dst, sem)
    copy.start()
    return copy


def begin_weights(win, wout, win_v, wout_v, sem):
    made = []
    for i in range(6):
        cols = pl.ds(512 * i, 512)
        made.append(begin(win.at[:, cols], win_v.at[:, cols], sem.at[i]))
    made.append(begin(wout, wout_v, sem.at[6]))
    return made


def shape(*dims, dtype=BF):
    return jax.ShapeDtypeStruct(dims, dtype)


def load_groups(x_ref, dst):
    for g in range(TOK // 12):
        dst[12 * g : 12 * g + 12, :] = x_ref[g].astype(F32)


def store_groups(src, out_ref):
    for g in range(TOK // 12):
        out_ref[g] = src[12 * g : 12 * g + 12, :].astype(BF)


def insert(piece_refs, pickt_ref):
    total = dot(pickt_ref[0], piece_refs[0][...])
    for q in range(1, 4):
        total = total + dot(pickt_ref[q], piece_refs[q][...])
    return total


def extract(value, pick_ref, out_refs):
    for q in range(4):
        out_refs[q][...] = dot(pick_ref[q], value).astype(BF)


def build_bias(kind, table_ref, oht_ref, rdiff, cdiff, out, tab, tops, mids, lows, tall, edge):
    tab[...] = jnp.zeros_like(tab)
    tab[:, :OFFSETS] = table_ref[...]
    for dl in range(3):
        for rq in range(6):
            for cq in range(12):
                start = LEVEL_STEP * dl + ROW_STEP * rq + cq
                at = ((dl * 6 + rq) * 12 + cq) * 16
                x = tab[:, start : start + 128]
                top = x.astype(BF)
                rest = x - top.astype(F32)
                mid = rest.astype(BF)
                tops[at : at + 16, :] = top
                mids[at : at + 16, :] = mid
                lows[at : at + 16, :] = (rest - mid.astype(F32)).astype(BF)
    for lq in range(2):
        for rq in range(6):
            one = ((1 + lq) * 6 + rq) * 192
            two = (lq * 6 + rq) * 192
            got = None
            for piece in (tops, mids, lows):
                x = jnp.concatenate([piece[one : one + 192, :], piece[two : two + 192, :]], axis=1)
                part = dot(x, oht_ref[...])
                got = part if got is None else got + part
            for cq in range(12):
                rows = pl.ds((lq * 6 + rq) * 12 + cq, 16, stride=WT)
                tall[rows, :] = got[cq * 16 : cq * 16 + 16, :128]
                edge[rows, :] = got[cq * 16 : cq * 16 + 16, 128:]
    split_rows = (kind[0] % 2).astype(F32)
    split_cols = (kind[0] // 2).astype(F32)
    closed = rdiff[...] * split_rows + cdiff[...] * split_cols > 0.0
    for h in range(HEADS):
        rows = slice(h * WT, h * WT + WT)
        out[rows, :128] = jnp.where(closed[:, :128], MASKED, tall[rows, :])
        out[rows, 128:] = jnp.where(closed[:, 128:], MASKED, edge[rows, : WT - 128])


def head_masks(scale):
    lane = lax.broadcasted_iota(jnp.int32, (1, 128), 1)
    low = jnp.where(lane < 64, scale, 0.0).astype(BF)
    high = jnp.where(lane >= 64, scale, 0.0).astype(BF)
    return low, high


def stacked(block, masks):
    return jnp.concatenate([block * masks[0], block * masks[1]], axis=0)


def norm_rows(xs, n_ref, at, count):
    x = xs[at : at + count, :]
    mean = jnp.mean(x, axis=-1, keepdims=True)
    centered = x - mean
    var = jnp.mean(centered * centered, axis=-1, keepdims=True)
    n_ref[at : at + count, :] = (centered * lax.rsqrt(var + NORM_EPS)).astype(BF)


def pair_lanes(p, base):
    return pl.ds(pl.multiple_of(base + p * 128, 128), 128)


def pair_rows(p):
    return pl.ds(pl.multiple_of(p * TOK, 8), TOK)


def forward_core(xs, win, wout, bias_ref, n_ref, c_ref, proj_ref, aug_ref, out, weights, bias_ready, made):
    for at in range(0, TOK, 48):
        norm_rows(xs, n_ref, at, 48)
    made("n")
    for i in range(6):
        weights[i].wait()
        cols = slice(512 * i, 512 * i + 512)
        proj_ref[:, cols] = dot(n_ref[...], win[:, cols]).astype(BF)
    made("proj")
    bias_ready()

    @pl.loop(0, PAIRS)
    def _(p):
        eighth = head_masks(0.125)
        ones = head_masks(1.0)
        lane = lax.broadcasted_iota(jnp.int32, (1, 128), 1)
        spot = lane % 64
        for w in range(MICRO):
            rows = slice(w * WT, w * WT + WT)
            qs = stacked(proj_ref[rows, pair_lanes(p, 0)], eighth)
            k = proj_ref[rows, pair_lanes(p, D)]
            v = proj_ref[rows, pair_lanes(p, 2 * D)]
            s = dot_nt(qs, k) + bias_ref[pair_rows(p), :]
            peak = jnp.max(s, axis=-1, keepdims=True)
            e = jnp.exp(s - peak).astype(BF)
            wide = [
                jnp.concatenate([v * one, jnp.broadcast_to(one, (WT, 128))], axis=1) for one in ones
            ]
            both = dot(e[:WT], wide[0]) + dot(e[WT:], wide[1])
            total = both[:, 128:]
            c_ref[rows, pair_lanes(p, 0)] = (both[:, :128] / total).astype(BF)
            lse = jnp.where(lane < 64, peak[:WT], peak[WT:]) + jnp.log(total)
            top = lse.astype(BF).astype(F32)
            mid = (lse - top).astype(BF).astype(F32)
            low = lse - top - mid
            aug = jnp.where(spot == 0, -top, jnp.where(spot == 1, -mid, jnp.where(spot == 2, -low, 0.0)))
            aug_ref[pl.ds(pl.multiple_of((p * 2 + w) * TOK, 16), TOK), :] = stacked(aug.astype(BF), ones)

    made("c")
    weights[6].wait()
    for c in range(0, D, 512):
        out[:, c : c + 512] = xs[:, c : c + 512] + dot(c_ref[...], wout[:, c : c + 512])


def backward_core(who, xs, go, win, wout, bias_ref, c_ref, proj_ref, aug_ref, oh_ref, gctx, gp, bacc, edge, fold, terms, out,
                  weights, ready, late_ref, late_sem):
    sent = []
    part = [lax.rem(who[1] + step, GROUP) for step in range(GROUP)]
    for step in range(GROUP):
        cols = pl.ds(pl.multiple_of(256 * part[step], 128), 256)
        sent.append(begin(go.at[:, cols], late_ref[step].at[pl.ds(0, TOK), pl.ds(768, 256)], late_sem.at[step, 0]))
    if weights:
        weights[6].wait()
    for c in range(0, D, 256):
        gctx[:, c : c + 256] = dot_nt(go[...], wout[c : c + 256, :]).astype(BF)
    edge[...] = jnp.zeros_like(edge)
    ready()

    @pl.loop(0, PAIRS)
    def _(p):
        eighth = head_masks(0.125)
        ones = head_masks(1.0)
        lane = lax.broadcasted_iota(jnp.int32, (1, 128), 1)
        fill = jnp.broadcast_to(jnp.where(lane % 64 < 3, 1.0, 0.0).astype(BF), (WT, 128))
        full = jnp.ones((WT, 128), BF)
        total = None
        for w in range(MICRO):
            rows = slice(w * WT, w * WT + WT)
            qs = stacked(proj_ref[rows, pair_lanes(p, 0)], eighth)
            k = proj_ref[rows, pair_lanes(p, D)]
            v = proj_ref[rows, pair_lanes(p, 2 * D)]
            aug = aug_ref[pl.ds(pl.multiple_of((p * 2 + w) * TOK, 16), TOK), :]
            s = dot_nt(jnp.concatenate([qs, aug], axis=1), jnp.concatenate([k, fill], axis=1))
            chances = jnp.exp(s + bias_ref[pair_rows(p), :])
            dc = gctx[rows, pair_lanes(p, 0)]
            dcs = stacked(dc, ones)
            along = -(dc.astype(F32) * c_ref[rows, pair_lanes(p, 0)].astype(F32))
            alongs = stacked(along.astype(BF), ones)
            slope = dot_nt(jnp.concatenate([dcs, alongs], axis=1), jnp.concatenate([v, full], axis=1))
            ds = chances * slope
            total = ds if total is None else total + ds
            dsb = ds.astype(BF)
            gp[rows, pair_lanes(p, 2 * D)] = dot_tn(chances.astype(BF), dcs).astype(BF)
            gp[rows, pair_lanes(p, D)] = dot_tn(dsb, qs).astype(BF)
            ks = [k * one for one in eighth]
            gp[rows, pair_lanes(p, 0)] = (dot(dsb[:WT], ks[0]) + dot(dsb[WT:], ks[1])).astype(BF)
        bacc[pair_rows(p), :] = total[:, :128]
        edge[pair_rows(p), : WT - 128] = total[:, 128:]

    for step in range(GROUP):
        cols = pl.ds(pl.multiple_of(768 * part[step], 128), 768)
        sent.append(begin(gp.at[:, cols], late_ref[step].at[pl.ds(0, TOK), pl.ds(0, 768)], late_sem.at[step, 1]))

    acc = [jnp.zeros((BIAS_ROWS, 256), F32) for _ in range(3)]
    blank = jnp.zeros((BIAS_ROWS, 128), F32)
    for rq in range(6):
        got = []
        for lq in range(2):
            taken = [pl.ds((lq * 6 + rq) * 12 + cq, 16, stride=WT) for cq in range(12)]
            x = jnp.concatenate(
                [jnp.concatenate([ref[rows, :] for rows in taken], axis=0) for ref in (bacc, edge)], axis=1
            )
            top = x.astype(BF)
            low = (x - top.astype(F32)).astype(BF)
            got.append(dot(top, oh_ref[...]) + dot(low, oh_ref[...]))
        levels = [got[0][:, 128:], got[0][:, :128] + got[1][:, 128:], got[1][:, :128]]
        for dl in range(3):
            for cq in range(12):
                one = jnp.concatenate([levels[dl][cq * 16 : cq * 16 + 16], blank], axis=1)
                shift = ROW_STEP * rq + cq
                acc[dl] = acc[dl] + (pltpu.roll(one, shift, 1) if shift else one)
    folded = jnp.zeros((BIAS_ROWS, D), F32)
    for dl in range(3):
        one = jnp.concatenate([acc[dl], jnp.zeros((BIAS_ROWS, D - 256), F32)], axis=1)
        folded = folded + (pltpu.roll(one, LEVEL_STEP * dl, 1) if dl else one)
    fold[...] = folded
    for step in range(GROUP):
        slab = fold[:, pl.ds(pl.multiple_of(256 * part[step], 128), 256)]
        top = slab.astype(BF)
        terms[step, :, :256] = top
        terms[step, :, 256:512] = (slab - top.astype(F32)).astype(BF)
        terms[step, :, 512:] = jnp.zeros((BIAS_ROWS, 512), BF)
        sent.append(begin(terms.at[step], late_ref[step].at[pl.ds(TOK, BIAS_ROWS), :], late_sem.at[step, 2]))

    if weights:
        for i in range(6):
            weights[i].wait()
    for c in range(0, D, 256):
        out[:, c : c + 256] = dot_nt(gp[...], win[c : c + 256, :]).astype(BF).astype(F32)
    for at in range(0, TOK, 48):
        rows = slice(at, at + 48)
        dn = out[rows, :]
        x = xs[rows, :]
        mean = jnp.mean(x, axis=-1, keepdims=True)
        centered = x - mean
        var = jnp.mean(centered * centered, axis=-1, keepdims=True)
        scale = lax.rsqrt(var + NORM_EPS)
        n = centered * scale
        along = jnp.mean(dn * n, axis=-1, keepdims=True)
        level = jnp.mean(dn, axis=-1, keepdims=True)
        dx = (scale * (dn - level - n * along)).astype(BF).astype(F32)
        out[rows, :] = go[rows, :].astype(F32) + dx
    return sent


def first_forward_body(who, kind, x_ref, table_ref, oht_ref, rdiff, cdiff, pick_ref, win, wout,
                       bias_out, nc_out, proj_out, aug_out, p0, p1, p2, p3,
                       win_v, wout_v, bias_v, n, c, proj, aug, xs, out, tab, tops, mids, lows, tall, edge, wsem, osem):
    @pl.when(who[0] == 0)
    def _():
        begin_weights(win, wout, win_v, wout_v, wsem)

    build_bias(kind, table_ref, oht_ref, rdiff, cdiff, bias_v, tab, tops, mids, lows, tall, edge)
    bias_copy = begin(bias_v, bias_out, osem.at[4])

    @pl.when(who[0] == 0)
    def _():
        weights = [
            pltpu.make_async_copy(win.at[:, pl.ds(512 * i, 512)], win_v.at[:, pl.ds(512 * i, 512)], wsem.at[i])
            for i in range(6)
        ] + [pltpu.make_async_copy(wout, wout_v, wsem.at[6])]
        load_groups(x_ref, xs)
        sent = []

        def made(name):
            if name == "n":
                sent.append(begin(n, nc_out.at[:, pl.ds(0, D)], osem.at[0]))
            if name == "proj":
                sent.append(begin(proj, proj_out, osem.at[1]))
            if name == "c":
                sent.append(begin(c, nc_out.at[:, pl.ds(D, D)], osem.at[2]))
                sent.append(begin(aug, aug_out, osem.at[3]))

        forward_core(xs, win_v, wout_v, bias_v, n, c, proj, aug, out, weights, lambda: None, made)
        extract(out[...].astype(BF), pick_ref, (p0, p1, p2, p3))
        for one in sent:
            one.wait()

    @pl.when(who[0] == 1)
    def _():
        load_groups(x_ref, xs)
        extract(xs[...].astype(BF), pick_ref, (p0, p1, p2, p3))

    bias_copy.wait()


def second_body(who, r0, r1, r2, r3, c0, c1, c2, c3, pick_ref, pickt_ref, oh_ref, bias_ref, win, wout,
                nc_out, l0, l1, l2, l3, s0, s1, s2, s3, g0, g1, g2, g3,
                win_v, wout_v, bias_v, c, proj, aug, xs, out, go, gctx, gp, bacc, edge, fold, terms,
                wsem, isem, lsem, n):
    @pl.when(who[0] == 1)
    def _():
        weights = begin_weights(win, wout, win_v, wout_v, wsem)
        bias_copy = begin(bias_ref, bias_v, isem.at[0])
        xs[...] = insert((r0, r1, r2, r3), pickt_ref)
        sent = []

        def made(name):
            if name == "n":
                sent.append(begin(n, nc_out.at[:, pl.ds(0, D)], isem.at[1]))
            if name == "c":
                sent.append(begin(c, nc_out.at[:, pl.ds(D, D)], isem.at[2]))

        forward_core(xs, win_v, wout_v, bias_v, n, c, proj, aug, out, weights, bias_copy.wait, made)
        extract(out[...].astype(BF), pick_ref, (s0, s1, s2, s3))
        go[...] = insert((c0, c1, c2, c3), pickt_ref).astype(BF)
        sent += backward_core(who, xs, go, win_v, wout_v, bias_v, c, proj, aug, oh_ref, gctx, gp, bacc, edge, fold, terms,
                              out, None, lambda: None, (l0, l1, l2, l3), lsem)
        extract(out[...].astype(BF), pick_ref, (g0, g1, g2, g3))
        for one in sent:
            one.wait()


def first_backward_body(who, x_ref, g0, g1, g2, g3, pickt_ref, oh_ref,
                        nc_ref, proj_ref, aug_ref, bias_ref, win, wout, b0, b1, b2, b3,
                        l0, l1, l2, l3, out_ref,
                        win_v, wout_v, bias_v, c, proj, aug, xs, out, go, gctx, gp, bacc, edge, fold, terms,
                        wsem, isem, lsem, hold):
    @pl.when(who[0] == 0)
    def _():
        weights = [None] * 7
        weights[6] = begin(wout, wout_v, wsem.at[6])
        copies = [
            begin(proj_ref, proj, isem.at[0]),
            begin(bias_ref, bias_v, isem.at[1]),
            begin(aug_ref, aug, isem.at[2]),
            begin(nc_ref.at[:, pl.ds(D, D)], c, isem.at[3]),
        ]
        for i in range(6):
            cols = pl.ds(512 * i, 512)
            weights[i] = begin(win.at[:, cols], win_v.at[:, cols], wsem.at[i])
        go[...] = insert((g0, g1, g2, g3), pickt_ref).astype(BF)
        load_groups(x_ref, xs)

        def ready():
            for one in copies:
                one.wait()

        sent = backward_core(who, xs, go, win_v, wout_v, bias_v, c, proj, aug, oh_ref, gctx, gp, bacc, edge, fold, terms,
                             out, weights, ready, (l0, l1, l2, l3), lsem)
        store_groups(out, out_ref)
        for one in sent:
            one.wait()

    @pl.when(who[0] == 1)
    def _():
        came = [begin(src, hold.at[j], lsem.at[j, 0]) for j, src in enumerate((b0, b1, b2, b3))]
        gone = []
        for j, dst in enumerate((l0, l1, l2, l3)):
            came[j].wait()
            gone.append(begin(hold.at[j], dst, lsem.at[j, 1]))
        for one in gone:
            one.wait()


def result_body(who, grad_ref, s0, s1, s2, s3, pickt_ref, out_ref, xs):
    @pl.when(who[0] == 0)
    def _():
        out_ref[...] = grad_ref[...]

    @pl.when(who[0] == 1)
    def _():
        xs[...] = insert((s0, s1, s2, s3), pickt_ref)
        store_groups(xs, out_ref)


def flip_body(who, *refs):
    early_a, early_b = refs[:GROUP], refs[GROUP : 2 * GROUP]
    out_ref, held, flipped, sem, osem = refs[2 * GROUP :]

    def copies(early):
        return [
            pltpu.make_async_copy(early[j], held.at[pl.ds(TOK * j, TOK)], sem.at[j]) for j in range(GROUP)
        ]

    @pl.when(who[0] == 0)
    def _():
        for one in copies(early_a):
            one.start()

    @pl.when(who[0] == 1)
    def _():
        for one in copies(early_b):
            one.start()

    for one in copies(early_a):
        one.wait()

    @pl.loop(0, 8)
    def _(i):
        at = pl.ds(pl.multiple_of(i * 256, 256), 256)
        flipped[at, :] = held[:, at].T
        pltpu.make_async_copy(flipped.at[at], out_ref.at[at], osem.at[i]).start()

    for i in range(8):
        at = pl.ds(i * 256, 256)
        pltpu.make_async_copy(flipped.at[at], out_ref.at[at], osem.at[i]).wait()


def weight_body(nct_ref, l0, l1, l2, l3, out_ref, nct, grads, terms, lsem, nsem):
    late = (l0, l1, l2, l3)
    copies = []
    for j in range(GROUP):
        copies.append(begin(late[j].at[pl.ds(0, TOK)], grads.at[pl.ds(TOK * j, TOK)], lsem.at[j, 0]))
        copies.append(begin(late[j].at[pl.ds(TOK, BIAS_ROWS)], terms.at[j], lsem.at[j, 1]))
    chunks = []
    for rb in range(4):
        for base in (0, D):
            rows = pl.ds(base + 256 * rb, 256)
            chunks.append(begin(nct_ref.at[rows], nct.at[rows], nsem.at[len(chunks)]))
    for one in copies:
        one.wait()

    slab = jnp.zeros((BIAS_ROWS, 256), F32)
    for j in range(GROUP):
        slab = slab + (terms[j, :, :256].astype(F32) + terms[j, :, 256:512].astype(F32))
    for half in range(2):
        piece = slab[:, half * 128 : half * 128 + 128].astype(BF)
        out_ref[:, 128 + half * 16 : 144 + half * 16, :] = jnp.broadcast_to(piece[None], (64, BIAS_ROWS, 128))

    for rb in range(4):
        dst = slice(rb * 16, rb * 16 + 16)
        chunks[2 * rb].wait()
        into = dot(nct[rb * 256 : rb * 256 + 256, :], grads[:, :768])
        for cb in range(6):
            out_ref[dst, cb * 16 : cb * 16 + 16, :] = into[:, cb * 128 : cb * 128 + 128].astype(BF).reshape(16, 16, 128)
        chunks[2 * rb + 1].wait()
        outof = dot(nct[D + rb * 256 : D + rb * 256 + 256, :], grads[:, 768:])
        for cb in range(2):
            out_ref[dst, 96 + cb * 16 : 112 + cb * 16, :] = outof[:, cb * 128 : cb * 128 + 128].astype(BF).reshape(16, 16, 128)


def sum_body(who, in_ref, w_ref, b_ref, bias):
    def fill(place):
        for part in range(GROUP):
            total = None
            for i in range(4):
                for xh in range(2):
                    for xl in range(2):
                        y, z = place(part, i)
                        one = in_ref[((y * 2 + xh) * 4 + z) * 2 + xl].astype(F32)
                        total = one if total is None else total + one
            for cb in range(6):
                w_ref[:, part * 768 + cb * 128 : part * 768 + cb * 128 + 128] = total[cb * 16 : cb * 16 + 16]
            for cb in range(2):
                at = 3 * D + part * 256 + cb * 128
                w_ref[:, at : at + 128] = total[96 + cb * 16 : 112 + cb * 16]
                bias[:, part * 256 + cb * 128 : part * 256 + cb * 128 + 128] = total[128 + cb * 16 : 144 + cb * 16]
        b_ref[...] = bias[:, :OFFSETS]

    @pl.when(who[0] == 0)
    def _():
        fill(lambda part, i: (i, part))

    @pl.when(who[0] == 1)
    def _():
        fill(lambda part, i: (part, i))


def per_device(boundary, tile_kinds, proj_in, proj_out, offset_bias):
    axes = ("lat", "lon", "section")
    nlat, nlon = lax.axis_size("lat"), lax.axis_size("lon")
    section = lax.axis_index("section")
    lat = lax.axis_index("lat")
    depth = jnp.where(section == 0, lat % GROUP, lat // (nlat // GROUP))
    who = jnp.stack([section, depth]).astype(jnp.int32)
    kind = tile_kinds.reshape(1)
    x = boundary.reshape(TOK // 12, 12, D)
    win = proj_in[0]
    wout = proj_out[0]
    onehot = jnp.asarray(ONEHOT, BF)
    onehot_t = jnp.asarray(ONEHOT.T, BF)
    pick = jnp.asarray(PICK, BF)
    pick_t = jnp.asarray(PICK.transpose(0, 2, 1), BF)

    def flat(lat, lon, sec):
        return ((lat % nlat) * nlon + lon % nlon) * 2 + sec

    def roll_pairs(dl, dn, from_section, to_section):
        return [
            (flat(i, j, from_section), flat(i + dl, j + dn, to_section))
            for i in range(nlat)
            for j in range(nlon)
        ]

    def forth(pieces, src, dst):
        got = []
        for dl in range(2):
            for dn in range(2):
                piece = pieces[(1 - dl) * 2 + (1 - dn)]
                if src == dst and dl == 0 and dn == 0:
                    got.append(piece)
                else:
                    got.append(lax.ppermute(piece, axes, roll_pairs(-dl, -dn, src, dst)))
        return got

    def back(pieces, src, dst):
        got = [None] * 4
        for dl in range(2):
            for dn in range(2):
                piece = pieces[dl * 2 + dn]
                if not (src == dst and dl == 0 and dn == 0):
                    piece = lax.ppermute(piece, axes, roll_pairs(dl, dn, src, dst))
                got[(1 - dl) * 2 + (1 - dn)] = piece
        return got

    def rings(stride, size, sec):
        chips = nlat * nlon
        return [
            [2 * (block + i + stride * m) + sec for m in range(GROUP)]
            for block in range(0, chips, size)
            for i in range(stride)
        ]

    z_rings = rings(nlon, GROUP * nlon, 0)
    y_rings = rings(nlat * nlon // GROUP, nlat * nlon, 1)

    def gather(value, groups):
        return [value] + [
            lax.ppermute(value, axes, [(g[m], g[(m + step) % GROUP]) for g in groups for m in range(GROUP)])
            for step in range(1, GROUP)
        ]

    def deal(values, groups):
        return [values[0]] + [
            lax.ppermute(values[step], axes, [(g[m], g[(m + step) % GROUP]) for g in groups for m in range(GROUP)])
            for step in range(1, GROUP)
        ]

    quarter = [shape(QT, D)] * 4
    f32 = functools.partial(shape, dtype=F32)
    vf32 = lambda *dims: pltpu.VMEM(dims, F32)
    vbf = lambda *dims: pltpu.VMEM(dims, BF)
    dma = lambda *dims: pltpu.SemaphoreType.DMA(dims)
    wide = shape(TOK, 3 * D)
    both = shape(TOK, 2 * D)
    augs = shape(PAIRS * MICRO * TOK, 128)
    late_shape = [shape(TOK + BIAS_ROWS, D)] * GROUP
    weights_v = [vbf(D, 3 * D), vbf(D, D), vf32(HEADS * WT, WT)]
    tall = [vf32(HEADS * WT, 128), vf32(HEADS * WT, 128)]
    pieces_v = [vbf(3 * 1152, 128)] * 3
    front_v = [vbf(TOK, D), vbf(TOK, D), vbf(TOK, 3 * D), vbf(PAIRS * MICRO * TOK, 128), vf32(TOK, D), vf32(TOK, D)]
    back_v = (
        weights_v
        + [vbf(TOK, D), vbf(TOK, 3 * D), vbf(PAIRS * MICRO * TOK, 128), vf32(TOK, D), vf32(TOK, D)]
        + [vbf(TOK, D), vbf(TOK, D), vbf(TOK, 3 * D)]
        + tall
        + [vf32(BIAS_ROWS, D), vbf(GROUP, BIAS_ROWS, D), dma(7), dma(4), dma(GROUP, 3)]
    )

    bias, nc_a, proj_a, aug_a, *pieces = call(
        first_forward_body, "first_forward", [f32(HEADS * WT, WT), both, wide, augs] + quarter,
        [SMEM, SMEM] + [VMEM] * 6 + [HBM] * 2,
        weights_v + front_v + [vf32(HEADS, OPAD)] + pieces_v + tall + [dma(7), dma(5)],
        5_000_000_000, 20_000_000, [HBM] * 4 + [VMEM] * 4,
    )(who, kind, x, offset_bias[0], onehot_t, jnp.asarray(ROWS_DIFFER), jnp.asarray(COLS_DIFFER), pick, win, wout)
    cots = forth(pieces, 1, 1)
    pieces, cots = lax.optimization_barrier((pieces, cots))
    received = forth(pieces, 0, 1)
    received, nc_a = lax.optimization_barrier((received, nc_a))
    early_a = gather(nc_a, z_rings)

    nc_b, *pieces = call(
        second_body, "second_both", [both] + late_shape + quarter * 2,
        [SMEM] + [VMEM] * 11 + [HBM] * 3,
        back_v + [vbf(TOK, D)], 12_000_000_000, 20_000_000, [HBM] * 5 + [VMEM] * 8,
    )(who, *received, *cots, pick, pick_t, onehot, bias, win, wout)
    late_b, second_out, grads = pieces[:4], pieces[4:8], pieces[8:]
    grads, early_a = lax.optimization_barrier((grads, early_a))
    grads = back(grads, 1, 0)
    grads, nc_b, second_out = lax.optimization_barrier((grads, nc_b, second_out))
    early_b = gather(nc_b, y_rings)

    *late, grad_in = call(
        first_backward_body, "first_backward", late_shape + [shape(TOK // 12, 12, D)],
        [SMEM] + [VMEM] * 7 + [HBM] * 10,
        back_v + [vbf(GROUP, TOK + BIAS_ROWS, D)], 8_000_000_000, 20_000_000, [HBM] * 4 + [VMEM],
    )(who, x, *grads, pick_t, onehot, nc_a, proj_a, aug_a, bias, win, wout, *late_b)
    grad_in, second_out = lax.optimization_barrier((grad_in, second_out))
    late = deal(late, z_rings + y_rings)
    second_out = back(second_out, 1, 1)

    flipped = call(
        flip_body, "flip", shape(2 * D, GROUP * TOK), [SMEM] + [HBM] * 8,
        [vbf(GROUP * TOK, 2 * D), vbf(2 * D, GROUP * TOK), dma(GROUP), dma(8)], 10_000_000, 10_000_000, HBM,
    )(who, *early_a, *early_b)
    result = call(
        result_body, "result", shape(TOK // 12, 12, D), [SMEM] + [VMEM] * 6, [vf32(TOK, D)], 170_000_000, 2_000_000,
        limit=SMALL,
    )(who, grad_in, *second_out, pick_t)

    terms = call(
        weight_body, "weight_terms", shape(64, 160, 128), [HBM] * 5,
        [vbf(2 * D, GROUP * TOK), vbf(GROUP * TOK, D), vbf(GROUP, BIAS_ROWS, D), dma(GROUP, 2), dma(8)],
        2_400_000_000, 10_000_000,
    )(flipped, *late)
    terms = lax.all_to_all(terms, ("lat", "lon"), 0, 0, tiled=True)

    weights, table = call(
        sum_body, "sum_terms", [f32(16, 4 * D), f32(HEADS, OFFSETS)], [SMEM, VMEM], [vf32(HEADS, D)], 3_000_000, 3_000_000,
        limit=SMALL,
    )(who, terms)
    return (result.reshape(boundary.shape), weights[None], table[None])


def solution(mesh):
    return jax.shard_map(
        per_device,
        mesh=mesh,
        in_specs=(
            P("section", None, None, "lat", "lon", None),
            P("section", "lat", "lon"),
            P("section", None, None),
            P("section", None, None),
            P("section", None, None),
        ),
        out_specs=(
            P("section", None, None, "lat", "lon", None),
            P("section", ("lat", "lon"), None),
            P("section", None, None),
        ),
        check_vma=False,
    )
```

time: 247 us -> 197 us (0.80)
  the two profiles are of different devices: /device:TPU:0 before, /device:TPU:1 now
where the time goes in v2:
time: 197 us; the launch traced here: 196 us
  starting transfers between devices  67.2 us (34%)
  waiting for transfers between devices  60.5 us (31%)
  Pallas kernels  59.1 us (30%)
  local copies, waits for them, and re-layouts  6.95 us (4%)
    pallas_call x1, Pallas kernels, per_device(): call(second_body, 'second_both', [both] + late_shape + quarter * 2, [SMEM...  28.9 us
    ppermute x7, waiting for transfers between devices, back(): piece = lax.ppermute(piece, axes, roll_pairs(dl, dn, src, dst))  26.7 us
    ppermute x7, starting transfers between devices, forth(): got.append(lax.ppermute(piece, axes, roll_pairs(-dl, -dn, src, dst)))  21.1 us
    ppermute x7, starting transfers between devices, back(): piece = lax.ppermute(piece, axes, roll_pairs(dl, dn, src, dst))  20.8 us
    ppermute x6, waiting for transfers between devices, gather(): lax.ppermute(value, axes, [(g[m], g[(m + step) % GROUP]) for g in groups...  15.9 us
    all_to_all x1, starting transfers between devices, per_device(): terms = lax.all_to_all(terms, ('lat', 'lon'), 0, 0, tiled=True)  10.9 us
    ppermute x7, waiting for transfers between devices, forth(): got.append(lax.ppermute(piece, axes, roll_pairs(-dl, -dn, src, dst)))  10.4 us
    pallas_call x1, Pallas kernels, per_device(): call(weight_body, 'weight_terms', shape(64, 160, 128), [HBM] * 5, [vbf(2...  9.81 us
  transfers between devices with their start and end apart: 24, of which 13 were waited for; matrix products, arithmetic and copies ran while one was open for 1% of the time, Pallas kernels for 21%

profile of v2, /device:TPU:1, one launch (start us, length us, event | category | flops | bytes accessed | tf_op | source)
XLA Modules:
  0.0 196.1 jit_solution(558949249582864217)
XLA Ops:
  1.3 2.1 %copy.14 = bf16[1,2,2,6,12,1024]{5,4,3,2,1,0:T(8,128)(2,1)} copy(bf16[1,2,2,6,12,1024]{5,2,4,3,1,0:T(2,128)(2,1)} %param.11) | data formatting | bytes 1179648 | tf_op args[0]
  4.0 6.4 %first_forward.1 = (f32[2304,144]{1,0:T(8,128)}, bf16[288,2048]{1,0:T(8,128)(2,1)}, bf16[288,3072]{1,0:T(8,128)(2,1)}, bf16[4608,128]{1,0:T(8,128)(2,1)}, bf16[7...) custom-call(s32[2]{0:T(128)} %pad_add_fusion.who, ...), custom_call_target="tpu_custom_call" | custom-call | flops 5000000000 | bytes 20000000 | tf_op jit(solution)/shard_map/first_forward/pallas_call | solution.py:645
  10.5 11.1 %collective-permute-start.2 = (bf16[72,1024]{1,0:T(8,128)(2,1)}, bf16[72,1024]{1,0:T(8,128)(2,1)S(1)}, u32[]{:S(2)}, u32[]{:S(2)}) collective-permute-start(bf16[72,1024]{1,0:T(8,128)(2,1)} %get-tuple-element.73), channel_id=1, source_target_pairs={{1,127},{3,125},{5,3},{7,1},{9,7},{11,5},{13,11},{15,9},{17,15},{1... | collective-permute-start | bytes 442376 | tf_op jit(solution)/shard_map/ppermute | solution.py:588
  21.6 2.9 %collective-permute-start.1 = (bf16[72,1024]{1,0:T(8,128)(2,1)}, bf16[72,1024]{1,0:T(8,128)(2,1)S(1)}, u32[]{:S(2)}, u32[]{:S(2)}) collective-permute-start(bf16[72,1024]{1,0:T(8,128)(2,1)} %get-tuple-element.72), channel_id=1, source_target_pairs={{1,125},{3,127},{5,1},{7,3},{9,5},{11,7},{13,9},{15,11},{17,13},{1... | collective-permute-start | bytes 442376 | tf_op jit(solution)/shard_map/ppermute | solution.py:588
  24.5 1.9 collective-permute-start
  27.7 2.9 %collective-permute-done.c1 = bf16[72,1024]{1,0:T(8,128)(2,1)S(1)} collective-permute-done((bf16[72,1024]{1,0:T(8,128)(2,1)}, bf16[72,1024]{1,0:T(8,128)(2,1)S(1)}, u32[]{:S(2)}, u32[]{:S(2)}) %collective-permute-start) | collective-permute-done | bytes 147488 | tf_op jit(solution)/shard_map/ppermute | solution.py:588
  35.9 2.8 %collective-permute-done.4.r1 = bf16[72,1024]{1,0:T(8,128)(2,1)S(1)} collective-permute-done((bf16[72,1024]{1,0:T(8,128)(2,1)}, bf16[72,1024]{1,0:T(8,128)(2,1)S(1)}, u32[]{:S(2)}, u32[]{:S(2)}) %collective-permute-start.4) | collective-permute-done | bytes 147488 | tf_op jit(solution)/shard_map/ppermute | solution.py:588
  39.9 2.2 %collective-permute-done.6.r3 = bf16[72,1024]{1,0:T(8,128)(2,1)S(1)} collective-permute-done((bf16[72,1024]{1,0:T(8,128)(2,1)}, bf16[72,1024]{1,0:T(8,128)(2,1)S(1)}, u32[]{:S(2)}, u32[]{:S(2)}) %collective-permute-start.6) | collective-permute-done | bytes 147488 | tf_op jit(solution)/shard_map/ppermute | solution.py:588
  44.4 28.9 %second_both.1 = (bf16[288,2048]{1,0:T(8,128)(2,1)}, bf16[304,1024]{1,0:T(8,128)(2,1)}, bf16[304,1024]{1,0:T(8,128)(2,1)}, bf16[304,1024]{1,0:T(8,128)(2,1)}, bf...) custom-call(s32[2]{0:T(128)} %pad_add_fusion.who, ...), custom_call_target="tpu_custom_call" | custom-call | flops 12000000000 | bytes 20000000 | tf_op jit(solution)/shard_map/second_both/pallas_call | solution.py:657
  73.4 5.8 %collective-permute-start.10 = (bf16[72,1024]{1,0:T(8,128)(2,1)}, bf16[72,1024]{1,0:T(8,128)(2,1)S(1)}, u32[]{:S(2)}, u32[]{:S(2)}) collective-permute-start(bf16[72,1024]{1,0:T(8,128)(2,1)} %get-tuple-element.89), channel_id=1, source_target_pairs={{1,6},{3,4},{5,10},{7,8},{9,14},{11,12},{13,18},{15,16},{17,22},{1... | collective-permute-start | bytes 442376 | tf_op jit(solution)/shard_map/ppermute | solution.py:597
  80.5 3.3 %collective-permute-start.12 = (bf16[72,1024]{1,0:T(8,128)(2,1)}, bf16[72,1024]{1,0:T(8,128)(2,1)S(1)}, u32[]{:S(2)}, u32[]{:S(2)}) collective-permute-start(bf16[72,1024]{1,0:T(8,128)(2,1)} %get-tuple-element.91), channel_id=1, source_target_pairs={{1,2},{3,0},{5,6},{7,4},{9,10},{11,8},{13,14},{15,12},{17,18},{19,... | collective-permute-start | bytes 442376 | tf_op jit(solution)/shard_map/ppermute | solution.py:597
  90.9 3.4 %collective-permute-start.17 = (bf16[288,2048]{1,0:T(8,128)(2,1)}, bf16[288,2048]{1,0:T(8,128)(2,1)}, u32[]{:S(2)}, u32[]{:S(2)}) collective-permute-start(bf16[288,2048]{1,0:T(8,128)(2,1)} %get-tuple-element.122.refs_4_), channel_id=1, source_target_pairs={{1,33},{33,65},{65,97},{97,1},{3,35},{35,67},{67,99},{99,3},{5,37}... | collective-permute-start | bytes 3538952 | tf_op jit(solution)/shard_map/ppermute | solution.py:614
  94.2 5.4 %first_backward.1 = (bf16[304,1024]{1,0:T(8,128)(2,1)}, bf16[304,1024]{1,0:T(8,128)(2,1)}, bf16[304,1024]{1,0:T(8,128)(2,1)}, bf16[304,1024]{1,0:T(8,128)(2,1)}, bf16[24,12,1024]{2,1,0:T(8,128)(2,1)}) custom-call(s32[2]{0:T(128)} %pad_add_fusion.who, bf16[24,12,1024]{2,1,0:T(8,128)(2,1)} %bitcast.13, bf16[72,1024]{1,0:T(8,128)(2,1)} %copy-done.17, ...), custom_call_target="tpu_custom_call" | custom-call | flops 8000000000 | bytes 20000000 | tf_op jit(solution)/shard_map/first_backward/pallas_call | solution.py:668
  100.9 2.5 %collective-permute-start.21 = (bf16[304,1024]{1,0:T(8,128)(2,1)}, bf16[304,1024]{1,0:T(8,128)(2,1)S(1)}, u32[]{:S(2)}, u32[]{:S(2)}) collective-permute-start(bf16[304,1024]{1,0:T(8,128)(2,1)} %get-tuple-element.125), channel_id=1, source_target_pairs={{0,8},{4,12},{8,0},{12,4},{2,10},{6,14},{10,2},{14,6},{16,24},{20,... | collective-permute-start | bytes 1867784 | tf_op jit(solution)/shard_map/ppermute | solution.py:620
  105.4 2.3 %collective-permute-done.18.refs_6_ = bf16[288,2048]{1,0:T(8,128)(2,1)S(1)} collective-permute-done((bf16[288,2048]{1,0:T(8,128)(2,1)}, bf16[288,2048]{1,0:T(8,128)(2,1)S(1)}, u32[]{:S(2)}, u32[]{:S(2)}) %collective-permute-start.18) | collective-permute-done | bytes 1179680 | tf_op jit(solution)/shard_map/ppermute | solution.py:614
  107.7 12.8 %collective-permute-done.17.refs_5_ = bf16[288,2048]{1,0:T(8,128)(2,1)} collective-permute-done((bf16[288,2048]{1,0:T(8,128)(2,1)}, bf16[288,2048]{1,0:T(8,128)(2,1)}, u32[]{:S(2)}, u32[]{:S(2)}) %collective-permute-start.17) | collective-permute-done | bytes 1179680 | tf_op jit(solution)/shard_map/ppermute | solution.py:614
  120.5 5.6 %flip.1.nct_ref = bf16[2048,1152]{1,0:T(8,128)(2,1)} custom-call(s32[2]{0:T(128)} %pad_add_fusion.who, bf16[288,2048]{1,0:T(8,128)(2,1)} %get-tuple-element.118.nc_ref.refs_0_, bf16[288,2048]{1,0:T(8,128)(2,1)} %copy-done.7, bf16[288,2048]{1,0:T(8,128)(2,1)} %copy-done.6, bf16[288,2048]{1,0:T(8,128)(2,1)} %copy-done.5, ...), custom_call_target="tpu_custom_call" | custom-call | flops 10000000 | bytes 10000000 | tf_op jit(solution)/shard_map/flip/pallas_call | solution.py:677
  127.2 6.4 %collective-permute-done.21.l2 = bf16[304,1024]{1,0:T(8,128)(2,1)S(1)} collective-permute-done((bf16[304,1024]{1,0:T(8,128)(2,1)}, bf16[304,1024]{1,0:T(8,128)(2,1)S(1)}, u32[]{:S(2)}, u32[]{:S(2)}) %collective-permute-start.21) | collective-permute-done | bytes 622624 | tf_op jit(solution)/shard_map/ppermute | solution.py:620
  134.7 9.8 %weight_terms.1 = bf16[64,160,128]{2,1,0:T(8,128)(2,1)} custom-call(bf16[2048,1152]{1,0:T(8,128)(2,1)} %flip.1.nct_ref, bf16[304,1024]{1,0:T(8,128)(2,1)} %get-tuple-element.123.l0, bf16[304,1024]{1,0:T(8,128)(2,1)} %copy-done.10, bf16[304,1024]{1,0:T(8,128)(2,1)} %copy-done.11, bf16[304,1024]{1,0:T(8,128)(2,1)} %copy-done.12), custom_call_target="tpu_custom_call" | custom-call | flops 2400000000 | bytes 10000000 | tf_op jit(solution)/shard_map/weight_terms/pallas_call | solution.py:686
  144.5 10.9 %all-to-all-start = ((bf16[64,160,128]{2,1,0:T(8,128)(2,1)}), bf16[64,160,128]{2,1,0:T(8,128)(2,1)S(1)}, u32[]{:S(2)}, u32[]{:S(2)}) async-start(bf16[64,160,128]{2,1,0:T(8,128)(2,1)} %weight_terms.1), calls=%async_computation | async-start | bytes 5242880 | tf_op jit(solution)/shard_map/all_to_all | solution.py:691
  155.4 3.8 %collective-permute-start.14 = (bf16[72,1024]{1,0:T(8,128)(2,1)}, bf16[72,1024]{1,0:T(8,128)(2,1)S(1)}, u32[]{:S(2)}, u32[]{:S(2)}) collective-permute-start(bf16[72,1024]{1,0:T(8,128)(2,1)} %get-tuple-element.114), channel_id=1, source_target_pairs={{1,7},{3,5},{5,11},{7,9},{9,15},{11,13},{13,19},{15,17},{17,23},{1... | collective-permute-start | bytes 442376 | tf_op jit(solution)/shard_map/ppermute | solution.py:597
  159.3 3.1 %collective-permute-start.15 = (bf16[72,1024]{1,0:T(8,128)(2,1)}, bf16[72,1024]{1,0:T(8,128)(2,1)S(1)}, u32[]{:S(2)}, u32[]{:S(2)}) collective-permute-start(bf16[72,1024]{1,0:T(8,128)(2,1)} %get-tuple-element.115), channel_id=1, source_target_pairs={{1,5},{3,7},{5,9},{7,11},{9,13},{11,15},{13,17},{15,19},{17,21},{1... | collective-permute-start | bytes 442376 | tf_op jit(solution)/shard_map/ppermute | solution.py:597
  162.4 2.2 %collective-permute-start.16 = (bf16[72,1024]{1,0:T(8,128)(2,1)}, bf16[72,1024]{1,0:T(8,128)(2,1)S(1)}, u32[]{:S(2)}, u32[]{:S(2)}) collective-permute-start(bf16[72,1024]{1,0:T(8,128)(2,1)} %get-tuple-element.116), channel_id=1, source_target_pairs={{1,3},{3,1},{5,7},{7,5},{9,11},{11,9},{13,15},{15,13},{17,19},{19,... | collective-permute-start | bytes 442376 | tf_op jit(solution)/shard_map/ppermute | solution.py:597
  164.6 25.5 %collective-permute-done.14.s0 = bf16[72,1024]{1,0:T(8,128)(2,1)S(1)} collective-permute-done((bf16[72,1024]{1,0:T(8,128)(2,1)}, bf16[72,1024]{1,0:T(8,128)(2,1)S(1)}, u32[]{:S(2)}, u32[]{:S(2)}) %collective-permute-start.14) | collective-permute-done | bytes 147488 | tf_op jit(solution)/shard_map/ppermute | solution.py:597
  (82 shorter events, 30.2 us)
Async XLA Ops:
  10.5 16.0 %collective-permute-start.2 = (bf16[72,1024]{1,0:T(8,128)(2,1)}, bf16[72,1024]{1,0:T(8,128)(2,1)S(1)}, u32[]{:S(2)}, u32[]{:S(2)}) collective-permute-start(bf16[72,1024]{1,0:T(8,128)(2,1)} %get-tuple-element.73), channel_id=1, source_target_pairs={{1,127},{3,125},{5,3},{7,1},{9,7},{11,5},{13,11},{15,9},{17,15},{1... | collective-permute-start | bytes 442376 | tf_op jit(solution)/shard_map/ppermute | solution.py:588
  21.6 6.1 %collective-permute-start.1 = (bf16[72,1024]{1,0:T(8,128)(2,1)}, bf16[72,1024]{1,0:T(8,128)(2,1)S(1)}, u32[]{:S(2)}, u32[]{:S(2)}) collective-permute-start(bf16[72,1024]{1,0:T(8,128)(2,1)} %get-tuple-element.72), channel_id=1, source_target_pairs={{1,125},{3,127},{5,1},{7,3},{9,5},{11,7},{13,9},{15,11},{17,13},{1... | collective-permute-start | bytes 442376 | tf_op jit(solution)/shard_map/ppermute | solution.py:588
  24.5 6.1 %collective-permute-start = (bf16[72,1024]{1,0:T(8,128)(2,1)}, bf16[72,1024]{1,0:T(8,128)(2,1)S(1)}, u32[]{:S(2)}, u32[]{:S(2)}) collective-permute-start(bf16[72,1024]{1,0:T(8,128)(2,1)} %get-tuple-element.71), channel_id=1, source_target_pairs={{1,3},{3,1},{5,7},{7,5},{9,11},{11,9},{13,15},{15,13},{17,19},{19,... | collective-permute-start | bytes 442376 | tf_op jit(solution)/shard_map/ppermute | solution.py:588
  30.6 5.2 %collective-permute-start.3 = (bf16[72,1024]{1,0:T(8,128)(2,1)}, bf16[72,1024]{1,0:T(8,128)(2,1)S(1)}, u32[]{:S(2)}, u32[]{:S(2)}) collective-permute-start(bf16[72,1024]{1,0:T(8,128)(2,1)} %get-tuple-element.79.c0), channel_id=1, source_target_pairs={{0,1},{2,3},{4,5},{6,7},{8,9},{10,11},{12,13},{14,15},{16,17},{18,... | collective-permute-start | bytes 442376 | tf_op jit(solution)/shard_map/ppermute | solution.py:588
  31.9 6.7 %collective-permute-start.4 = (bf16[72,1024]{1,0:T(8,128)(2,1)}, bf16[72,1024]{1,0:T(8,128)(2,1)S(1)}, u32[]{:S(2)}, u32[]{:S(2)}) collective-permute-start(bf16[72,1024]{1,0:T(8,128)(2,1)} %get-tuple-element.71), channel_id=1, source_target_pairs={{0,3},{2,1},{4,7},{6,5},{8,11},{10,9},{12,15},{14,13},{16,19},{18,... | collective-permute-start | bytes 442376 | tf_op jit(solution)/shard_map/ppermute | solution.py:588
  33.2 6.7 %collective-permute-start.5 = (bf16[72,1024]{1,0:T(8,128)(2,1)}, bf16[72,1024]{1,0:T(8,128)(2,1)S(1)}, u32[]{:S(2)}, u32[]{:S(2)}) collective-permute-start(bf16[72,1024]{1,0:T(8,128)(2,1)} %get-tuple-element.72), channel_id=1, source_target_pairs={{0,125},{2,127},{4,1},{6,3},{8,5},{10,7},{12,9},{14,11},{16,13},{1... | collective-permute-start | bytes 442376 | tf_op jit(solution)/shard_map/ppermute | solution.py:588
  34.5 7.6 %collective-permute-start.6 = (bf16[72,1024]{1,0:T(8,128)(2,1)}, bf16[72,1024]{1,0:T(8,128)(2,1)S(1)}, u32[]{:S(2)}, u32[]{:S(2)}) collective-permute-start(bf16[72,1024]{1,0:T(8,128)(2,1)} %get-tuple-element.73), channel_id=1, source_target_pairs={{0,127},{2,125},{4,3},{6,1},{8,7},{10,5},{12,11},{14,9},{16,15},{1... | collective-permute-start | bytes 442376 | tf_op jit(solution)/shard_map/ppermute | solution.py:588
  42.1 31.2 %collective-permute-start.9 = (bf16[288,2048]{1,0:T(8,128)(2,1)}, bf16[288,2048]{1,0:T(8,128)(2,1)S(1)}, u32[]{:S(2)}, u32[]{:S(2)}) collective-permute-start(bf16[288,2048]{1,0:T(8,128)(2,1)} %get-tuple-element.118.nc_ref.refs_0_), channel_id=1, source_target_pairs={{0,12},{4,0},{8,4},{12,8},{2,14},{6,2},{10,6},{14,10},{16,28},{20,... | collective-permute-start | bytes 3538952 | tf_op jit(solution)/shard_map/ppermute | solution.py:614
  42.8 30.5 %collective-permute-start.8 = (bf16[288,2048]{1,0:T(8,128)(2,1)}, bf16[288,2048]{1,0:T(8,128)(2,1)S(1)}, u32[]{:S(2)}, u32[]{:S(2)}) collective-permute-start(bf16[288,2048]{1,0:T(8,128)(2,1)} %get-tuple-element.118.nc_ref.refs_0_), channel_id=1, source_target_pairs={{0,8},{4,12},{8,0},{12,4},{2,10},{6,14},{10,2},{14,6},{16,24},{20,... | collective-permute-start | bytes 3538952 | tf_op jit(solution)/shard_map/ppermute | solution.py:614
  43.6 29.8 %collective-permute-start.7 = (bf16[288,2048]{1,0:T(8,128)(2,1)}, bf16[288,2048]{1,0:T(8,128)(2,1)S(1)}, u32[]{:S(2)}, u32[]{:S(2)}) collective-permute-start(bf16[288,2048]{1,0:T(8,128)(2,1)} %get-tuple-element.118.nc_ref.refs_0_), channel_id=1, source_target_pairs={{0,4},{4,8},{8,12},{12,0},{2,6},{6,10},{10,14},{14,2},{16,20},{20,... | collective-permute-start | bytes 3538952 | tf_op jit(solution)/shard_map/ppermute | solution.py:614
  73.4 11.7 %collective-permute-start.10 = (bf16[72,1024]{1,0:T(8,128)(2,1)}, bf16[72,1024]{1,0:T(8,128)(2,1)S(1)}, u32[]{:S(2)}, u32[]{:S(2)}) collective-permute-start(bf16[72,1024]{1,0:T(8,128)(2,1)} %get-tuple-element.89), channel_id=1, source_target_pairs={{1,6},{3,4},{5,10},{7,8},{9,14},{11,12},{13,18},{15,16},{17,22},{1... | collective-permute-start | bytes 442376 | tf_op jit(solution)/shard_map/ppermute | solution.py:597
  79.2 5.9 %collective-permute-start.11 = (bf16[72,1024]{1,0:T(8,128)(2,1)}, bf16[72,1024]{1,0:T(8,128)(2,1)S(1)}, u32[]{:S(2)}, u32[]{:S(2)}) collective-permute-start(bf16[72,1024]{1,0:T(8,128)(2,1)} %get-tuple-element.90), channel_id=1, source_target_pairs={{1,4},{3,6},{5,8},{7,10},{9,12},{11,14},{13,16},{15,18},{17,20},{1... | collective-permute-start | bytes 442376 | tf_op jit(solution)/shard_map/ppermute | solution.py:597
  80.5 5.7 %collective-permute-start.12 = (bf16[72,1024]{1,0:T(8,128)(2,1)}, bf16[72,1024]{1,0:T(8,128)(2,1)S(1)}, u32[]{:S(2)}, u32[]{:S(2)}) collective-permute-start(bf16[72,1024]{1,0:T(8,128)(2,1)} %get-tuple-element.91), channel_id=1, source_target_pairs={{1,2},{3,0},{5,6},{7,4},{9,10},{11,8},{13,14},{15,12},{17,18},{19,... | collective-permute-start | bytes 442376 | tf_op jit(solution)/shard_map/ppermute | solution.py:597
  83.9 2.5 %collective-permute-start.13 = (bf16[72,1024]{1,0:T(8,128)(2,1)}, bf16[72,1024]{1,0:T(8,128)(2,1)S(1)}, u32[]{:S(2)}, u32[]{:S(2)}) collective-permute-start(bf16[72,1024]{1,0:T(8,128)(2,1)} %get-tuple-element.92), channel_id=1, source_target_pairs={{1,0},{3,2},{5,4},{7,6},{9,8},{11,10},{13,12},{15,14},{17,16},{19,... | collective-permute-start | bytes 442376 | tf_op jit(solution)/shard_map/ppermute | solution.py:597
  87.0 17.1 %collective-permute-start.19 = (bf16[288,2048]{1,0:T(8,128)(2,1)}, bf16[288,2048]{1,0:T(8,128)(2,1)S(1)}, u32[]{:S(2)}, u32[]{:S(2)}) collective-permute-start(bf16[288,2048]{1,0:T(8,128)(2,1)} %get-tuple-element.122.refs_4_), channel_id=1, source_target_pairs={{1,97},{33,1},{65,33},{97,65},{3,99},{35,3},{67,35},{99,67},{5,101... | collective-permute-start | bytes 3538952 | tf_op jit(solution)/shard_map/ppermute | solution.py:614
  88.9 18.8 %collective-permute-start.18 = (bf16[288,2048]{1,0:T(8,128)(2,1)}, bf16[288,2048]{1,0:T(8,128)(2,1)S(1)}, u32[]{:S(2)}, u32[]{:S(2)}) collective-permute-start(bf16[288,2048]{1,0:T(8,128)(2,1)} %get-tuple-element.122.refs_4_), channel_id=1, source_target_pairs={{1,65},{33,97},{65,1},{97,33},{3,67},{35,99},{67,3},{99,35},{5,69}... | collective-permute-start | bytes 3538952 | tf_op jit(solution)/shard_map/ppermute | solution.py:614
  90.9 29.7 %collective-permute-start.17 = (bf16[288,2048]{1,0:T(8,128)(2,1)}, bf16[288,2048]{1,0:T(8,128)(2,1)}, u32[]{:S(2)}, u32[]{:S(2)}) collective-permute-start(bf16[288,2048]{1,0:T(8,128)(2,1)} %get-tuple-element.122.refs_4_), channel_id=1, source_target_pairs={{1,33},{33,65},{65,97},{97,1},{3,35},{35,67},{67,99},{99,3},{5,37}... | collective-permute-start | bytes 3538952 | tf_op jit(solution)/shard_map/ppermute | solution.py:614
  99.6 27.6 %collective-permute-start.20 = (bf16[304,1024]{1,0:T(8,128)(2,1)}, bf16[304,1024]{1,0:T(8,128)(2,1)S(1)}, u32[]{:S(2)}, u32[]{:S(2)}) collective-permute-start(bf16[304,1024]{1,0:T(8,128)(2,1)} %get-tuple-element.124), channel_id=1, source_target_pairs={{0,4},{4,8},{8,12},{12,0},{2,6},{6,10},{10,14},{14,2},{16,20},{20,... | collective-permute-start | bytes 1867784 | tf_op jit(solution)/shard_map/ppermute | solution.py:620
  100.9 32.7 %collective-permute-start.21 = (bf16[304,1024]{1,0:T(8,128)(2,1)}, bf16[304,1024]{1,0:T(8,128)(2,1)S(1)}, u32[]{:S(2)}, u32[]{:S(2)}) collective-permute-start(bf16[304,1024]{1,0:T(8,128)(2,1)} %get-tuple-element.125), channel_id=1, source_target_pairs={{0,8},{4,12},{8,0},{12,4},{2,10},{6,14},{10,2},{14,6},{16,24},{20,... | collective-permute-start | bytes 1867784 | tf_op jit(solution)/shard_map/ppermute | solution.py:620
  104.2 29.5 %collective-permute-start.22 = (bf16[304,1024]{1,0:T(8,128)(2,1)}, bf16[304,1024]{1,0:T(8,128)(2,1)S(1)}, u32[]{:S(2)}, u32[]{:S(2)}) collective-permute-start(bf16[304,1024]{1,0:T(8,128)(2,1)} %get-tuple-element.126), channel_id=1, source_target_pairs={{0,12},{4,0},{8,4},{12,8},{2,14},{6,2},{10,6},{14,10},{16,28},{20,... | collective-permute-start | bytes 1867784 | tf_op jit(solution)/shard_map/ppermute | solution.py:620
  144.5 50.0 %all-to-all-start = ((bf16[64,160,128]{2,1,0:T(8,128)(2,1)}), bf16[64,160,128]{2,1,0:T(8,128)(2,1)S(1)}, u32[]{:S(2)}, u32[]{:S(2)}) async-start(bf16[64,160,128]{2,1,0:T(8,128)(2,1)} %weight_terms.1), calls=%async_computation | async-start | bytes 5242880 | tf_op jit(solution)/shard_map/all_to_all | solution.py:691
  155.4 34.7 %collective-permute-start.14 = (bf16[72,1024]{1,0:T(8,128)(2,1)}, bf16[72,1024]{1,0:T(8,128)(2,1)S(1)}, u32[]{:S(2)}, u32[]{:S(2)}) collective-permute-start(bf16[72,1024]{1,0:T(8,128)(2,1)} %get-tuple-element.114), channel_id=1, source_target_pairs={{1,7},{3,5},{5,11},{7,9},{9,15},{11,13},{13,19},{15,17},{17,23},{1... | collective-permute-start | bytes 442376 | tf_op jit(solution)/shard_map/ppermute | solution.py:597
  159.3 30.8 %collective-permute-start.15 = (bf16[72,1024]{1,0:T(8,128)(2,1)}, bf16[72,1024]{1,0:T(8,128)(2,1)S(1)}, u32[]{:S(2)}, u32[]{:S(2)}) collective-permute-start(bf16[72,1024]{1,0:T(8,128)(2,1)} %get-tuple-element.115), channel_id=1, source_target_pairs={{1,5},{3,7},{5,9},{7,11},{9,13},{11,15},{13,17},{15,19},{17,21},{1... | collective-permute-start | bytes 442376 | tf_op jit(solution)/shard_map/ppermute | solution.py:597
  162.4 27.7 %collective-permute-start.16 = (bf16[72,1024]{1,0:T(8,128)(2,1)}, bf16[72,1024]{1,0:T(8,128)(2,1)S(1)}, u32[]{:S(2)}, u32[]{:S(2)}) collective-permute-start(bf16[72,1024]{1,0:T(8,128)(2,1)} %get-tuple-element.116), channel_id=1, source_target_pairs={{1,3},{3,1},{5,7},{7,5},{9,11},{11,9},{13,15},{15,13},{17,19},{19,... | collective-permute-start | bytes 442376 | tf_op jit(solution)/shard_map/ppermute | solution.py:597
  (24 other events, 299.1 us)
